TPU v7x, 512 devices: a whole 4x8x8 slice. The times are simulated.
512 devices in a mesh: feat: 64 (over z_hi, y, x), head: 8 (over z_lo, core).
Axes of the slice: x: 4, y: 8, z: 8 (z_hi: 2, z_lo: 4; z = z_hi * 4 + z_lo), core: 2. Of those that a mesh axis runs over, the one named last changes fastest.
Arguments:
- target_grads: bfloat16 [32, 5376], P('head', 'feat'), may hold values from -6 to 6
- positions: int32 [32], replicated, may hold values from 0 to 255
- raw_patterns: float32 [32, 32, 256], P('head'), may hold values from 0.02 to 1
- out_proj: bfloat16 [4096, 5376], P('head', 'feat'), may hold values from -0.078125 to 0.078125
- value_proj: bfloat16 [4096, 5376], P('head', 'feat'), may hold values from -0.5 to 0.5
- decoders: bfloat16 [24576, 5376], P('feat'), may hold values from -0.078125 to 0.078125
- feature_ids: int32 [256, 64], replicated, may hold values from 0 to 24575
- activations: float32 [256, 64], replicated, may hold values from 0.1 to 4
Outputs:
- edges: float32 [32, 256, 64], P('head')
All inputs are finite; a program needn't handle non-finite values.
Results may differ from a plain program's by a relative error of at most 0.0044.
Values may be sent and summed in bfloat16 or wider, within the bound.
A program may use at most 128 MiB of HBM per device.

v0:
```python
import jax
import jax.numpy as jnp
from jax import lax
from jax.sharding import PartitionSpec as P

HD = 128
S = 256


def body(
    target_grads, positions, raw_patterns, out_proj, value_proj, decoders, feature_ids, activations
):
    own_count = target_grads.shape[0]
    width_here = target_grads.shape[1]
    heads_here = out_proj.shape[0] // HD
    feat_here = decoders.shape[0]
    all_grads = lax.all_gather(target_grads, "head", axis=0, tiled=True)
    total_rows = all_grads.shape[0]
    partial_in = jnp.dot(all_grads, out_proj.T, preferred_element_type=jnp.float32)
    head_in = lax.psum(partial_in, "feat").astype(jnp.bfloat16)
    through = jnp.einsum(
        "the,hed->thd",
        head_in.reshape(total_rows, heads_here, HD),
        value_proj.reshape(heads_here, HD, width_here),
        preferred_element_type=jnp.float32,
    )
    spots = jnp.arange(S, dtype=jnp.int32)
    causal = (spots[None, :] <= positions[:, None]).astype(jnp.float32)
    masked = raw_patterns * causal[None, :, :]
    pattern = masked / jnp.sum(masked, axis=2, keepdims=True)
    first_row = lax.axis_index("head") * own_count
    attended = jnp.einsum("hts,thd->tsd", pattern, through, precision=lax.Precision.HIGHEST)
    summed = lax.psum(attended, "head")
    own_attended = lax.dynamic_slice_in_dim(summed, first_row, own_count, 0)
    own_positions = lax.dynamic_slice_in_dim(positions, first_row, own_count, 0)
    direct = (spots[None, :] == own_positions[:, None]).astype(jnp.float32)
    panel = (
        own_attended + direct[:, :, None] * target_grads.astype(jnp.float32)[:, None, :]
    ).astype(jnp.bfloat16)
    first_feat = lax.axis_index("feat") * feat_here
    local_ids = feature_ids - first_feat
    owned = (local_ids >= 0) & (local_ids < feat_here)
    clipped = jnp.clip(local_ids, 0, feat_here - 1)
    full_panel = lax.all_gather(panel, "feat", axis=2, tiled=True)
    flat_panel = full_panel.reshape(own_count * S, full_panel.shape[2])
    scores = jnp.dot(flat_panel, decoders.T, preferred_element_type=jnp.float32)
    scores = scores.reshape(own_count, S, feat_here)
    picked = jnp.take_along_axis(scores, clipped[None, :, :], axis=2)
    part_edges = jnp.where(owned[None, :, :], picked * activations[None, :, :], 0.0)
    return lax.psum(part_edges, "feat")


def solution(mesh):
    placed = (
        P("head", "feat"),
        P(),
        P("head", None, None),
        P("head", "feat"),
        P("head", "feat"),
        P("feat", None),
        P(),
        P(),
    )
    return jax.shard_map(
        body, mesh=mesh, in_specs=placed, out_specs=P("head", None, None), check_vma=False
    )
```

profile of v0, /device:TPU:60, one launch (start us, length us, event | category | flops | bytes accessed | tf_op | source)
XLA Modules:
  0.0 2093.8 jit_solution(1320275581053414654)
XLA Ops:
  6.5 0.8 fusion.9
  7.3 1.0 multiply_reduce_fusion
  8.3 1.0 multiply_divide_fusion
  9.3 14.6 all-gather
  23.9 0.1 fusion.11
  24.1 420.9 %psum.21 = bf16[32,512]{1,0:T(8,128)(2,1)S(1)} all-reduce(f32[32,512]{1,0:T(8,128)S(1)} %fusion.11), channel_id=1, replica_groups=mesh['feat'=64,'head'=8] {'feat'}, use_global_device_ids=true, to_apply=%region_1.0 | all-reduce | flops 16384 | bytes 98304 | tf_op jit(solution)/shard_map/psum | solution.py:20
  444.9 0.9 reshape.76
  445.9 0.1 convolution_bitcast_fusion
  446.0 4.1 fusion.3
  450.2 0.7 convert_element_type.26
  450.9 0.7 dynamic_slice.7
  451.7 97.3 %all-reduce.3.cloned.1.call-done = f32[32,256,84]{1,2,0:T(8,128)} async-done(((f32[32,256,84]{1,2,0:T(8,128)}), f32[32,256,84]{1,2,0:T(8,128)}) %all-reduce.3.cloned.1.call-update) | async-done | bytes 2752528 | tf_op jit(solution)/shard_map/psum | solution.py:33
  549.0 1.1 add_convert_fusion
  550.1 0.7 copy.18
  550.9 0.9 bitcast_or_fusion
  551.8 0.1 copy.20
  552.0 228.4 %all-gather.3.cloned.1.call-done = bf16[4,256,5376]{1,0,2:T(4,128)(2,1)} async-done(((bf16[4,256,84]{1,0,2:T(4,128)(2,1)}), bf16[4,256,5376]{1,0,2:T(4,128)(2,1)}) %all-gather.3.cloned.1.call-update) | async-done | bytes 11010064 | tf_op jit(solution)/shard_map/all_gather | solution.py:44
  780.4 10.0 fusion
  790.4 24.7 %copy.21 = f32[4,256,384]{0,2,1:T(8,128)} copy(f32[4,256,384]{2,1,0:T(8,128)S(1)} %fusion) | data formatting | bytes 3145728 | tf_op jit(solution)/shard_map/dot_general | solution.py:46
  815.1 362.6 %gather_fusion = f32[16384,4]{1,0:T(8,128)} fusion(f32[4,256,384]{0,2,1:T(8,128)} %copy.21, s32[16384]{0:T(1024)S(1)} %reshape.78), kind=kCustom, calls=%fused_computation | custom fusion | bytes 655360 | tf_op jit(solution)/shard_map/jit(take_along_axis)/gather | solution.py:48
  1177.7 6.4 copy.22
  1184.1 0.7 select_bitcast_fusion
  1184.8 900.8 %all-reduce.5.cloned.1.call-done = f32[4,256,64]{1,2,0:T(8,128)} async-done(((f32[4,256,64]{1,2,0:T(8,128)}), f32[4,256,64]{1,2,0:T(8,128)}) %all-reduce.5.cloned.1.call-update) | async-done | bytes 262160 | tf_op jit(solution)/shard_map/psum | solution.py:50
  2085.6 1.7 copy.38
  (17 shorter events, 0.4 us)
Async XLA Ops:
  6.5 17.4 copy-start
  6.5 545.4 %copy-start.2 = (s32[256,64]{0,1:T(8,128)S(1)}, s32[256,64]{0,1:T(8,128)}, u32[]{:S(2)}) copy-start(s32[256,64]{0,1:T(8,128)} %param.14) | copy-start | bytes 196612
  6.5 542.5 %all-reduce.3.cloned.1.call-start = ((), (), s32[]{:S(2)}) async-start(), calls=%async_computation | async-start | bytes 5767168 | tf_op jit(solution)/shard_map/psum | solution.py:33
  450.2 330.2 %all-gather.3.cloned.1.call-start = ((), (), s32[]{:S(2)}) async-start(), calls=%async_computation.1 | async-start | bytes 11182080 | tf_op jit(solution)/shard_map/all_gather | solution.py:44
  550.9 1534.8 %all-reduce.5.cloned.1.call-start = ((), (), s32[]{:S(2)}) async-start(), calls=%async_computation.2 | async-start | bytes 524288 | tf_op jit(solution)/shard_map/psum | solution.py:50
  790.4 1296.9 %copy-start.1 = (bf16[512,84]{0,1:T(8,128)(2,1)S(1)}, bf16[512,84]{0,1:T(8,128)(2,1)}, u32[]{:S(2)}) copy-start(bf16[512,84]{0,1:T(8,128)(2,1)} %param.11) | copy-start | bytes 258052
  815.1 369.0 %copy-start.3 = (f32[256,64]{0,1:T(8,128)S(1)}, f32[256,64]{0,1:T(8,128)}, u32[]{:S(2)}) copy-start(f32[256,64]{0,1:T(8,128)} %param.15) | copy-start | bytes 196612
Sparse Core Ops, SparseCore 0:
  450.3 98.6 all-reduce.2
  553.5 226.8 all-gather.2
  1184.9 900.6 all-reduce.4
where the time goes:
time: 2100 us; the launch traced here: 2090 us
  waiting for transfers between devices  1230 us (59%)
  blocking collectives  435 us (21%)
  local copies, waits for them, and re-layouts  398 us (19%)
    psum x1, waiting for transfers between devices, body(): return lax.psum(part_edges, 'feat')  901 us
    psum x1, blocking collectives, body(): head_in = lax.psum(partial_in, 'feat').astype(jnp.bfloat16)  421 us
    gather x4, local copies, waits for them, and re-layouts, body(): picked = jnp.take_along_axis(scores, clipped[None, :, :], axis=2)  369 us
    all_gather x1, waiting for transfers between devices, body(): full_panel = lax.all_gather(panel, 'feat', axis=2, tiled=True)  228 us
    psum x1, waiting for transfers between devices, body(): summed = lax.psum(attended, 'head')  97.3 us
  transfers between devices with their start and end apart: 3, of which 3 were waited for; matrix products, arithmetic and copies ran while one was open for 0% of the time, Pallas kernels for 0%

commit v1 on v0

v1 whole, which is shorter than its diff:
```python
import functools

import jax
import jax.numpy as jnp
from jax import lax
from jax.experimental import pallas as pl
from jax.experimental.pallas import tpu as pltpu
from jax.sharding import PartitionSpec as P

MESH = pl.DeviceIdType.MESH
HD = 128
NZ, NY, NX, NH = 2, 8, 4, 8
NT = (((1,), (1,)), ((), ()))


def dot(a, b, dims=(((1,), (0,)), ((), ()))):
    return lax.dot_general(a, b, dims, preferred_element_type=jnp.float32)


def kernel(
    nz, ny, nx, nh, stop,
    pos_ref, grads_ref, raw_ref, outp_ref, valp_ref, dec_hbm, ids_ref, act_ref,
    out_ref,
    dec, gall, ga, gy, gfull, pall, psend, part, rs, ex, hall, tsend, tall, ablk, thr,
    eparts, ers, e1, eex, fin,
    dec_sem, ssem, rsem, ring_s, ring_r,
):
    f32, bf16 = jnp.float32, jnp.bfloat16
    na = nz * nx
    w = grads_ref.shape[1]
    wx = nx * w
    tokens = ids_ref.shape[0]
    feats = dec.shape[0]
    rows = nh * 16
    f = lax.axis_index("feat")
    g = lax.axis_index("head")
    x = lax.rem(f, nx)
    y = lax.rem(lax.div(f, nx), ny)
    z = lax.div(f, nx * ny)
    a = z * nx + x

    def head_at(d):
        j = lax.rem(g + d, nh)
        return j, (f, j)

    def y_at(d):
        j = lax.rem(y + d, ny)
        return j, (z * (nx * ny) + j * nx + x, g)

    def a_at(d):
        j = lax.rem(a + d, na)
        return j, (lax.div(j, nx) * (nx * ny) + y * nx + lax.rem(j, nx), g)

    groups = {"h": (head_at, nh), "y": (y_at, ny), "a": (a_at, na)}

    barrier = pltpu.get_barrier_semaphore()
    for at, n in groups.values():
        for d in range(1, n):
            pl.semaphore_signal(barrier, inc=1, device_id=at(d)[1], device_id_type=MESH)

    dec_copy = pltpu.make_async_copy(dec_hbm, dec, dec_sem)
    dec_copy.start()

    def exchange(stage, group, src, dst):
        at, n = groups[group]
        copies = []
        for d in range(1, n):
            j, device = at(d)
            copy = pltpu.make_async_remote_copy(
                src_ref=src(j),
                dst_ref=dst(d),
                send_sem=ssem.at[stage, d],
                recv_sem=rsem.at[stage, d],
                device_id=device,
                device_id_type=MESH,
            )
            copy.start()
            copies.append(copy)
        return copies

    def arrive(copies):
        for copy in copies:
            copy.wait_recv()

    pending = []

    own = grads_ref[...].astype(f32)
    mine = jnp.concatenate([own, own], axis=0)
    zero_lanes = jnp.zeros((8, gall.shape[2]), f32)
    gall[g] = zero_lanes
    gall[g, :, 0:w] = mine
    ga[a] = zero_lanes
    ga[a, :, 0:w] = mine
    pl.semaphore_wait(barrier, nh - 1 + ny - 1 + na - 1)
    c0 = exchange(0, "h", lambda j: gall.at[g], lambda d: gall.at[g])
    c2 = exchange(2, "a", lambda j: ga.at[a], lambda d: ga.at[a])

    for j in range(nh):
        for h in range(4):
            psend[j, 4 * h : 4 * h + 4, :] = raw_ref[h, 4 * j : 4 * j + 4, :]
    c1 = exchange(1, "h", lambda j: psend.at[j], lambda d: pall.at[g])
    pall[g] = psend[g]
    tsend[...] = jnp.zeros_like(tsend)

    arrive(c0)
    both = gall[...].reshape(nh * 8, gall.shape[2])[:, 0:w]
    low = lax.rem(lax.broadcasted_iota(jnp.int32, both.shape, 0), 8) < 4
    half = 2 * HD
    partial = dot(jnp.where(low, both, 0.0).astype(bf16), outp_ref[0:half, :], NT)
    partial += dot(jnp.where(low, 0.0, both).astype(bf16), outp_ref[half : 2 * half, :], NT)
    part[...] = partial.reshape(ny, 8, half)
    c4 = exchange(4, "y", lambda j: part.at[j], lambda d: rs.at[d])

    arrive(c2)
    for k in range(nz):
        for i in range(nx):
            gy[y, k, :, w * i : w * i + w] = ga[k * nx + i, :, 0:w]
    c3 = exchange(3, "y", lambda j: gy.at[y], lambda d: gy.at[y])

    arrive(c4)
    total = part[y]
    for d in range(1, ny):
        total += rs[d]
    ex[0] = total
    c5 = exchange(5, "a", lambda j: ex.at[0], lambda d: ex.at[d])
    arrive(c5)
    for d in range(1, na):
        total += ex[d]
    hall[y] = total.astype(bf16).astype(f32)
    c6 = exchange(6, "y", lambda j: hall.at[y], lambda d: hall.at[y])

    arrive(c1)
    raw = pall[...].reshape(rows, tokens)
    row_t = lax.rem(lax.broadcasted_iota(jnp.int32, raw.shape, 0), 4)
    spot = lax.broadcasted_iota(jnp.int32, raw.shape, 1)
    row_pos = jnp.zeros(raw.shape, jnp.int32)
    own_pos = []
    for t in range(4):
        own_pos.append(pos_ref[4 * g + t])
        row_pos = jnp.where(row_t == t, own_pos[t], row_pos)
    masked = jnp.where(spot <= row_pos, raw, 0.0)
    pattern = masked / jnp.sum(masked, axis=1, keepdims=True)
    pat = pattern.T
    pat_hi = pat.astype(bf16)
    pat_lo = (pat - pat_hi.astype(f32)).astype(bf16)

    arrive(c3)
    for k in range(nz):
        for j in range(ny):
            at = wx * (k * ny + j)
            gfull[:, at : at + wx] = gy[j, k, :, 0:wx]

    arrive(c6)
    hin = hall[...].reshape(ny * 8, half).astype(bf16)
    r = lax.broadcasted_iota(jnp.int32, (rows, ny * 8), 0)
    c = lax.broadcasted_iota(jnp.int32, (rows, ny * 8), 1)
    from_row = lax.div(r, 16) * 8 + lax.div(lax.rem(r, 16), 8) * 4 + lax.rem(r, 4)
    spread = dot((c == from_row).astype(bf16), hin)
    r = lax.broadcasted_iota(jnp.int32, (rows, half), 0)
    lane = lax.broadcasted_iota(jnp.int32, (rows, half), 1)
    fits = lax.rem(lax.div(r, 4), 2) == lax.div(lane, HD)
    upper = lax.rem(lax.div(r, 8), 2) == 1
    first = jnp.where(fits & ~upper, spread, 0.0).astype(bf16)
    second = jnp.where(fits & upper, spread, 0.0).astype(bf16)
    through = dot(first, valp_ref[0:half, :]) + dot(second, valp_ref[half : 2 * half, :])
    tsend[:, :, 0:w] = through.astype(bf16).reshape(nh, 16, w)
    c7 = exchange(7, "h", lambda j: tsend.at[j], lambda d: tall.at[g])
    tall[g] = tsend[g]

    dec_copy.wait()
    straight = dot(gfull[...].astype(bf16), dec[...], NT)

    arrive(c7)
    turned = tall[...].reshape(rows, tall.shape[2]).astype(f32).T
    ablk[a] = turned[0 : ablk.shape[1]].astype(bf16)
    c8 = exchange(8, "a", lambda j: ablk.at[a], lambda d: ablk.at[a])
    arrive(c8)
    for k in range(nz):
        joined = [ablk[k * nx + i].astype(f32)[0:w] for i in range(nx)]
        thr[k, y] = jnp.concatenate(joined, axis=0).astype(bf16)

    def hop(way, step, k):
        origin = lax.rem(y + (ny - step if way == 0 else step), ny)
        return pltpu.make_async_remote_copy(
            src_ref=thr.at[k, origin],
            dst_ref=thr.at[k, origin],
            send_sem=ring_s.at[way, step, k],
            recv_sem=ring_r.at[way, step, k],
            device_id=y_at(1 if way == 0 else ny - 1)[1],
            device_id_type=MESH,
        )

    def ring_has(way, step, k):
        if step < ny // 2 - 1:
            return True
        return step == ny // 2 - 1 and k == way

    hops = {}
    for step in range(ny // 2):
        for k in range(nz):
            for way in range(2):
                if not ring_has(way, step, k):
                    continue
                if step > 0:
                    hops[way, step - 1, k].wait_recv()
                hops[way, step, k] = hop(way, step, k)
                hops[way, step, k].start()
    for (way, step, k), copy in hops.items():
        if not ring_has(way, step + 1, k):
            copy.wait_recv()

    span = ny * wx
    scores = dot(dec[:, 0:span], thr[0].reshape(span, rows))
    for k in range(1, nz):
        scores += dot(dec[:, k * span : (k + 1) * span], thr[k].reshape(span, rows))
    sc_hi = scores.astype(bf16)
    sc_lo = (scores - sc_hi.astype(f32)).astype(bf16)
    right = jnp.concatenate([sc_hi, sc_hi, sc_lo], axis=1)

    ids = ids_ref[...] - f * feats
    ids = jnp.concatenate([ids, ids], axis=1)
    act = act_ref[...]
    act = jnp.concatenate([act, act], axis=1)
    lane = lax.broadcasted_iota(jnp.int32, ids.shape, 1)
    of_t = lax.rem(lax.broadcasted_iota(jnp.int32, pat.shape, 1), 4)
    token = lax.broadcasted_iota(jnp.int32, (tokens, feats), 0)
    piece = tokens // ny
    for p in range(2):
        picked = []
        for q in range(2):
            t = 2 * p + q
            hi = jnp.where(of_t == t, pat_hi, 0.0)
            lo = jnp.where(of_t == t, pat_lo, 0.0)
            left = jnp.concatenate([hi, lo, hi], axis=1)
            table = dot(left, right, NT)
            table += jnp.where(token == own_pos[t], straight[t : t + 1, :], 0.0)
            found = jnp.zeros(ids.shape, f32)
            for b in range(feats // 128):
                local = ids - 128 * b
                inside = (local >= 0) & (local < 128)
                taken = jnp.take_along_axis(
                    table[:, 128 * b : 128 * b + 128], jnp.clip(local, 0, 127), axis=1
                )
                found = jnp.where(inside, taken, found)
            picked.append(found)
        edge = jnp.where(lane < 64, picked[0], picked[1]) * act
        edge = edge.astype(bf16)
        for j in range(ny):
            eparts[j, p] = edge[piece * j : piece * (j + 1)]

    c10 = exchange(10, "y", lambda j: eparts.at[j], lambda d: ers.at[d])
    arrive(c10)
    total = eparts[y].astype(f32)
    for d in range(1, ny):
        total += ers[d].astype(f32)
    e1[...] = total.astype(bf16)
    c11 = exchange(11, "a", lambda j: e1, lambda d: eex.at[d])
    arrive(c11)
    for d in range(1, na):
        total += eex[d].astype(f32)
    fin[y] = total.astype(bf16)
    c12 = exchange(12, "y", lambda j: fin.at[y], lambda d: fin.at[y])
    arrive(c12)
    for j in range(ny):
        for p in range(2):
            block = fin[j, p].astype(f32)
            out_ref[2 * p, piece * j : piece * (j + 1), :] = block[:, 0:64]
            out_ref[2 * p + 1, piece * j : piece * (j + 1), :] = block[:, 64:128]

    for copies in (c0, c1, c2, c3, c4, c5, c6, c7, c8, c10, c11, c12):
        for copy in copies:
            copy.wait_send()
    for copy in hops.values():
        copy.wait_send()


def body(nz, ny, nx, nh, stop, grads, positions, raw, out_proj, value_proj, decoders, ids, act):
    f32, bf16 = jnp.float32, jnp.bfloat16
    w = grads.shape[1]
    tokens, listed = ids.shape
    feats, width = decoders.shape
    na, rows, piece = nz * nx, nh * 16, tokens // ny
    wx = nx * w
    lanes_w = -(-w // 128) * 128
    lanes_x = -(-wx // 128) * 128
    tall_w = -(-w // 16) * 16
    vmem = pltpu.VMEM
    scratch = [
        vmem((feats, width), bf16),
        vmem((nh, 8, lanes_w), f32),
        vmem((na, 8, lanes_w), f32),
        vmem((ny, nz, 8, lanes_x), f32),
        vmem((8, width), f32),
        vmem((nh, 16, tokens), f32),
        vmem((nh, 16, tokens), f32),
        vmem((ny, 8, 2 * HD), f32),
        vmem((ny, 8, 2 * HD), f32),
        vmem((na, 8, 2 * HD), f32),
        vmem((ny, 8, 2 * HD), f32),
        vmem((nh, 16, lanes_w), bf16),
        vmem((nh, 16, lanes_w), bf16),
        vmem((na, tall_w, rows), bf16),
        vmem((nz, ny, wx, rows), bf16),
        vmem((ny, 2, piece, 2 * listed), bf16),
        vmem((ny, 2, piece, 2 * listed), bf16),
        vmem((2, piece, 2 * listed), bf16),
        vmem((na, 2, piece, 2 * listed), bf16),
        vmem((ny, 2, piece, 2 * listed), bf16),
        pltpu.SemaphoreType.DMA,
        pltpu.SemaphoreType.DMA((13, 8)),
        pltpu.SemaphoreType.DMA((13, 8)),
        pltpu.SemaphoreType.DMA((2, max(ny // 2, 1), nz)),
        pltpu.SemaphoreType.DMA((2, max(ny // 2, 1), nz)),
    ]
    in_vmem = pl.BlockSpec(memory_space=pltpu.VMEM)
    return pl.pallas_call(
        functools.partial(kernel, nz, ny, nx, nh, stop),
        out_shape=jax.ShapeDtypeStruct((4, tokens, listed), f32),
        in_specs=[pl.BlockSpec(memory_space=pltpu.SMEM)]
        + [in_vmem] * 4
        + [pl.BlockSpec(memory_space=pl.ANY)]
        + [in_vmem] * 2,
        out_specs=in_vmem,
        scratch_shapes=scratch,
        compiler_params=pltpu.CompilerParams(
            collective_id=0, has_side_effects=True, vmem_limit_bytes=40 * 1024 * 1024
        ),
    )(positions, grads, raw, out_proj, value_proj, decoders, ids, act)


def solution(mesh, sizes=(NZ, NY, NX, NH), stop=99):
    placed = (
        P("head", "feat"),
        P(),
        P("head", None, None),
        P("head", "feat"),
        P("head", "feat"),
        P("feat", None),
        P(),
        P(),
    )
    return jax.shard_map(
        functools.partial(body, *sizes, stop),
        mesh=mesh,
        in_specs=placed,
        out_specs=P("head", None, None),
        check_vma=False,
    )
```

time: 2100 us -> 97.9 us (0.05)
  the two profiles are of different devices: /device:TPU:60 before, /device:TPU:8 now
where the time goes in v1:
time: 97.9 us; the launch traced here: 97.5 us
  Pallas kernels  88.2 us (90%)
  local copies, waits for them, and re-layouts  9.21 us (9%)
    pallas_call x1, Pallas kernels, body(): pl.pallas_call(functools.partial(kernel, nz, ny, nx, nh, stop), out_shape...  88.2 us
    unnamed x12, local copies, waits for them, and re-layouts  8.32 us

profile of v1, /device:TPU:8, one launch (start us, length us, event | category | flops | bytes accessed | tf_op | source)
XLA Modules:
  0.0 97.5 jit_solution(11549857456056933023)
XLA Ops:
  0.0 1.0 %copy.9.outp_ref = bf16[512,84]{1,0:T(8,128)(2,1)S(1)} copy(bf16[512,84]{0,1:T(8,128)(2,1)} %param.11) | data formatting | bytes 172032 | tf_op args[3]
  1.0 1.0 %copy.10.valp_ref = bf16[512,84]{1,0:T(8,128)(2,1)S(1)} copy(bf16[512,84]{0,1:T(8,128)(2,1)} %param.12) | data formatting | bytes 172032 | tf_op args[4]
  2.1 0.9 copy.11.ids_ref
  3.0 0.9 copy.12.act_ref
  3.9 0.0 copy-start
  3.9 2.2 %copy-done = bf16[384,5376]{1,0:T(8,128)(2,1)S(1)} copy-done((bf16[384,5376]{1,0:T(8,128)(2,1)S(1)}, bf16[384,5376]{1,0:T(8,128)(2,1)}, u32[]{:S(2)}) %copy-start) | copy-done | bytes 4128792
  6.1 0.0 copy-start.1
  6.1 0.9 copy-done.1
  7.0 0.0 copy-start.2
  7.0 0.7 copy-done.2
  7.7 0.0 copy-start.3
  7.7 0.7 copy-done.3
  8.3 88.2 %shard_map.82 = f32[4,256,64]{2,1,0:T(8,128)S(1)} custom-call(s32[32]{0:T(128)S(1)} %copy-done.3, bf16[4,84]{1,0:T(4,128)(2,1)S(1)} %copy-done.2, f32[4,32,256]{2,1,0:T(8,128)S(1)} %copy-done.1, bf16[512,84]{1,0:T(8,128)(2,1)S(1)} %copy.9.outp_ref, bf16[512,84]{1,0:T(8,128)(2,1)S(1)} %copy.10.valp_ref, bf16[384,5376]{1,0:T(8,128)(2,1)S(1)} %copy-done, ...), custom_call_target="tpu_custom_call" | custom-call | tf_op jit(solution)/shard_map/pallas_call | solution.py:316
  96.6 0.9 copy.13
Async XLA Ops:
  3.9 2.2 %copy-start = (bf16[384,5376]{1,0:T(8,128)(2,1)S(1)}, bf16[384,5376]{1,0:T(8,128)(2,1)}, u32[]{:S(2)}) copy-start(bf16[384,5376]{1,0:T(8,128)(2,1)} %dec_hbm.1) | copy-start | bytes 12386308
  6.1 0.9 copy-start.1
  7.0 0.7 copy-start.2
  7.7 0.7 copy-start.3

commit v2 on v1

v2 whole, which is shorter than its diff:
```python
import functools

import jax
import jax.numpy as jnp
from jax import lax
from jax.experimental import pallas as pl
from jax.experimental.pallas import tpu as pltpu
from jax.sharding import PartitionSpec as P

MESH = pl.DeviceIdType.MESH
HD = 128
NZ, NY, NX, NH = 2, 8, 4, 8
NT = (((1,), (1,)), ((), ()))


def dot(a, b, dims=(((1,), (0,)), ((), ()))):
    return lax.dot_general(a, b, dims, preferred_element_type=jnp.float32)


def kernel(
    nz, ny, nx, nh, stop,
    pos_ref, grads_ref, raw_hbm, outp_hbm, valp_hbm, dec_hbm, ids_hbm, act_hbm,
    out_ref,
    raw_ref, outp_ref, valp_ref, ids_ref, act_ref, dec, gall, ga, gy, gfull, pall, psend, part, rs, ex, hall, tsend, tall, ax, bx, thr,
    eparts, ers, e1, eex, fin, pats, ids_t,
    in_sem, ssem, rsem, side_s, side_r,
):
    f32, bf16 = jnp.float32, jnp.bfloat16
    na = nz * nx
    w = grads_ref.shape[1]
    wx = nx * w
    listed, tokens = ids_ref.shape
    feats = dec.shape[0]
    rows = nh * 16
    f = lax.axis_index("feat")
    g = lax.axis_index("head")
    x = lax.rem(f, nx)
    y = lax.rem(lax.div(f, nx), ny)
    z = lax.div(f, nx * ny)
    a = z * nx + x

    def head_at(d):
        j = lax.rem(g + d, nh)
        return j, (f, j)

    def y_at(d):
        j = lax.rem(y + d, ny)
        return j, (z * (nx * ny) + j * nx + x, g)

    def a_at(d):
        j = lax.rem(a + d, na)
        return j, (lax.div(j, nx) * (nx * ny) + y * nx + lax.rem(j, nx), g)

    def x_at(d):
        j = lax.rem(x + d, nx)
        return j, (f - x + j, g)

    def z_at(d):
        j = lax.rem(z + d, nz)
        return j, (f + (j - z) * (nx * ny), g)

    groups = {"h": (head_at, nh), "y": (y_at, ny), "a": (a_at, na), "x": (x_at, nx)}

    barrier = pltpu.get_barrier_semaphore()
    for name in ("h", "y", "a"):
        at, n = groups[name]
        for d in range(1, n):
            pl.semaphore_signal(barrier, inc=1, device_id=at(d)[1], device_id_type=MESH)

    loads = {}
    for i, (name, src, dst) in enumerate(
        (
            ("raw", raw_hbm, raw_ref),
            ("outp", outp_hbm, outp_ref),
            ("valp", valp_hbm, valp_ref.at[z]),
            ("ids", ids_hbm, ids_ref),
            ("act", act_hbm, act_ref),
            ("dec", dec_hbm, dec),
        )
    ):
        loads[name] = pltpu.make_async_copy(src, dst, in_sem.at[i])
        loads[name].start()

    def load(name):
        loads[name].wait()
        loaded.append(name)

    def exchange(stage, group, src, dst):
        at, n = groups[group]
        copies = []
        for d in range(1, n):
            j, device = at(d)
            copy = pltpu.make_async_remote_copy(
                src_ref=src(j),
                dst_ref=dst(d),
                send_sem=ssem.at[stage, d],
                recv_sem=rsem.at[stage, d],
                device_id=device,
                device_id_type=MESH,
            )
            copy.start()
            copies.append(copy)
            started.append(copy)
        return copies

    def send(slot, src, dst, device):
        copy = pltpu.make_async_remote_copy(
            src_ref=src,
            dst_ref=dst,
            send_sem=side_s.at[slot],
            recv_sem=side_r.at[slot],
            device_id=device,
            device_id_type=MESH,
        )
        copy.start()
        started.append(copy)
        return copy

    def arrive(copies):
        for copy in copies:
            copy.wait_recv()
            arrived.append(copy)

    def finish():
        for copy in started:
            if not any(copy is other for other in arrived):
                copy.wait_recv()
            copy.wait_send()
        for name, copy in loads.items():
            if name not in loaded:
                copy.wait()

    started, arrived, loaded = [], [], []

    own = grads_ref[...].astype(f32)
    mine = jnp.concatenate([own, own], axis=0)
    zero_lanes = jnp.zeros((8, gall.shape[2]), f32)
    gall[g] = zero_lanes
    gall[g, :, 0:w] = mine
    ga[a] = zero_lanes
    ga[a, :, 0:w] = mine
    pl.semaphore_wait(barrier, nh - 1 + ny - 1 + na - 1)
    c0 = exchange(0, "h", lambda j: gall.at[g], lambda d: gall.at[g])
    load("valp")
    cv = send(0, valp_ref.at[z], valp_ref.at[z], z_at(1)[1])

    load("raw")
    for j in range(nh):
        for h in range(4):
            psend[j, 4 * h : 4 * h + 4, :] = raw_ref[h, 4 * j : 4 * j + 4, :]
    tsend[...] = jnp.zeros_like(tsend)
    load("outp")

    arrive(c0)
    if stop <= 0:
        return finish()
    both = gall[...].reshape(nh * 8, gall.shape[2])[:, 0:w]
    low = lax.rem(lax.broadcasted_iota(jnp.int32, both.shape, 0), 8) < 4
    half = 2 * HD
    partial = dot(jnp.where(low, both, 0.0).astype(bf16), outp_ref[:, 0:half])
    partial += dot(jnp.where(low, 0.0, both).astype(bf16), outp_ref[:, half : 2 * half])
    part[...] = partial.reshape(ny, 8, half)
    c4 = exchange(4, "y", lambda j: part.at[j], lambda d: rs.at[d])
    c1 = exchange(1, "h", lambda j: psend.at[j], lambda d: pall.at[g])
    pall[g] = psend[g]
    c2 = exchange(2, "a", lambda j: ga.at[a], lambda d: ga.at[a])

    arrive(c4)
    if stop <= 4:
        return finish()
    total = part[y]
    for d in range(1, ny):
        total += rs[d]
    ex[0] = total
    c5 = exchange(5, "a", lambda j: ex.at[0], lambda d: ex.at[d])

    arrive(c2)
    for k in range(nz):
        for i in range(nx):
            gy[y, k, :, w * i : w * i + w] = ga[k * nx + i, :, 0:w]

    r = lax.broadcasted_iota(jnp.int32, (rows, ny * 8), 0)
    c = lax.broadcasted_iota(jnp.int32, (rows, ny * 8), 1)
    from_row = lax.div(r, 16) * 8 + lax.div(lax.rem(r, 16), 8) * 4 + lax.rem(r, 4)
    choose = (c == from_row).astype(bf16)
    r = lax.broadcasted_iota(jnp.int32, (rows, half), 0)
    lane = lax.broadcasted_iota(jnp.int32, (rows, half), 1)
    fits = lax.rem(lax.div(r, 4), 2) == lax.div(lane, HD)
    upper = lax.rem(lax.div(r, 8), 2) == 1

    arrive(c5)
    if stop <= 5:
        return finish()
    for d in range(1, na):
        total += ex[d]
    hall[y] = total.astype(bf16).astype(f32)
    c6 = exchange(6, "y", lambda j: hall.at[y], lambda d: hall.at[y])

    arrive(c1)
    raw = pall[...].reshape(rows, tokens)
    row_t = lax.rem(lax.broadcasted_iota(jnp.int32, raw.shape, 0), 4)
    spot = lax.broadcasted_iota(jnp.int32, raw.shape, 1)
    row_pos = jnp.zeros(raw.shape, jnp.int32)
    own_pos = []
    for t in range(4):
        own_pos.append(pos_ref[4 * g + t])
        row_pos = jnp.where(row_t == t, own_pos[t], row_pos)
    masked = jnp.where(spot <= row_pos, raw, 0.0)
    pattern = masked / jnp.sum(masked, axis=1, keepdims=True)
    pat = pattern.T
    pat_hi = pat.astype(bf16)
    pat_lo = (pat - pat_hi.astype(f32)).astype(bf16)
    pats[0] = pat_hi
    pats[1] = pat_lo

    arrive([cv])
    arrive(c6)
    if stop <= 6:
        return finish()
    hin = hall[...].reshape(ny * 8, half).astype(bf16)
    spread = dot(choose, hin)
    first = jnp.where(fits & ~upper, spread, 0.0).astype(bf16)
    second = jnp.where(fits & upper, spread, 0.0).astype(bf16)
    for k in range(nz):
        through = dot(first, valp_ref[k, :, 0:half], NT)
        through += dot(second, valp_ref[k, :, half : 2 * half], NT)
        tsend[:, k, :, 0:w] = through.astype(bf16).reshape(nh, 16, w)
    c7 = exchange(7, "h", lambda j: tsend.at[j], lambda d: tall.at[g])
    tall[g] = tsend[g]
    c3 = exchange(3, "y", lambda j: gy.at[y], lambda d: gy.at[y])

    load("ids")
    load("act")
    ids = ids_ref[...] - f * feats
    ids_t[...] = jnp.concatenate([ids, ids], axis=0).T

    arrive(c7)
    if stop <= 7:
        return finish()
    tall_w = ax.shape[1]

    def turned(k):
        block = tall[:, k].reshape(rows, tall.shape[3]).astype(f32).T
        return block[0:tall_w].astype(bf16)

    ax[x] = turned(0)
    cx = exchange(8, "x", lambda j: ax.at[x], lambda d: ax.at[x])
    bx[x, 0] = turned(1)
    cy = exchange(9, "y", lambda j: bx.at[x, 0], lambda d: bx.at[x, d])
    right, left = x_at(1)[1], x_at(nx - 1)[1]
    from_left, from_right = x_at(nx - 1)[0], x_at(1)[0]
    hops = {}

    def pass_on(d):
        hops["r", d] = send(20 + 2 * d, bx.at[x, d], bx.at[x, d], right)
        hops["l", d] = send(21 + 2 * d, bx.at[x, d], bx.at[x, d], left)

    pass_on(0)
    arrive(cx)
    joined = [ax[i].astype(f32)[0:w] for i in range(nx)]
    thr[0, y] = jnp.concatenate(joined, axis=0).astype(bf16)
    mine_y = thr.at[0, y]
    far = {}
    steps = (2, ny - 2, 1, ny - 1) if ny == 8 else (1,)
    for i, d in enumerate(steps):
        far[d] = send(1 + i, mine_y, mine_y, y_at(d)[1])
    order = (1, ny - 1, 2, ny - 2, 3, ny - 3, 4) if ny == 8 else (1,)
    for d in order:
        arrive([cy[d - 1]])
        pass_on(d)

    load("dec")
    arrive(c3)
    for k in range(nz):
        for j in range(ny):
            at = wx * (k * ny + j)
            gfull[:, at : at + wx] = gy[j, k, :, 0:wx]

    cut = (wx // 32) * 16
    if ny == 8:
        arrive([far[2]])
        back = thr.at[0, y_at(ny - 2)[0]]
        far[3] = send(5, back, back, y_at(1)[1])
        back = thr.at[0, y_at(ny - 2)[0], 0:cut]
        far["low"] = send(6, back, back, y_at(2)[1])
        arrive([far[ny - 2]])
        back = thr.at[0, y_at(2)[0]]
        far[ny - 3] = send(7, back, back, y_at(ny - 1)[1])
        back = thr.at[0, y_at(2)[0], cut:wx]
        far["high"] = send(8, back, back, y_at(ny - 2)[1])
    for d in (0,) + order:
        arrive([hops["r", d]])
        if d <= ny // 2 - 1:
            hops["r2", d] = send(40 + d, bx.at[from_left, d], bx.at[from_left, d], right)
        arrive([hops["l", d]])
        if d > ny // 2 - 1:
            hops["l2", d] = send(40 + d, bx.at[from_right, d], bx.at[from_right, d], left)

    straight = dot(gfull[...].astype(bf16), dec[...], NT)

    for d in far:
        if not any(far[d] is other for other in arrived):
            arrive([far[d]])
    span = ny * wx
    scores = dot(dec[:, 0:span], thr[0].reshape(span, rows))
    for d in range(ny):
        arrive([hops["r2" if d <= ny // 2 - 1 else "l2", d]])
    if stop <= 9:
        return finish()
    for d in range(ny):
        joined = [bx[i, d].astype(f32)[0:w] for i in range(nx)]
        thr[1, y_at(ny - d)[0]] = jnp.concatenate(joined, axis=0).astype(bf16)
    scores += dot(dec[:, span : 2 * span], thr[1].reshape(span, rows))
    sc_hi = scores.astype(bf16)
    sc_lo = (scores - sc_hi.astype(f32)).astype(bf16)
    right = jnp.concatenate([sc_hi, sc_hi, sc_lo], axis=1)

    ids = ids_t[...]
    act = act_ref[...]
    act = jnp.concatenate([act, act], axis=0)
    lane = lax.broadcasted_iota(jnp.int32, ids.shape, 1)
    pat_hi, pat_lo = pats[0], pats[1]
    of_t = lax.rem(lax.broadcasted_iota(jnp.int32, pat_hi.shape, 1), 4)
    token = lax.broadcasted_iota(jnp.int32, (tokens, feats), 0)
    piece = 2 * listed // ny
    for p in range(2):
        picked = []
        for q in range(2):
            t = 2 * p + q
            hi = jnp.where(of_t == t, pat_hi, 0.0)
            lo = jnp.where(of_t == t, pat_lo, 0.0)
            left = jnp.concatenate([hi, lo, hi], axis=1)
            table = dot(left, right, NT)
            table += jnp.where(token == own_pos[t], straight[t : t + 1, :], 0.0)
            found = jnp.zeros(ids.shape, f32)
            for b in range(feats // 128):
                local = ids - 128 * b
                inside = (local >= 0) & (local < 128)
                taken = jnp.take_along_axis(
                    table[:, 128 * b : 128 * b + 128], jnp.clip(local, 0, 127), axis=1
                )
                found = jnp.where(inside, taken, found)
            picked.append(found)
        edge = jnp.where(lane < listed, picked[0], picked[1]).T * act
        edge = edge.astype(bf16)
        for j in range(ny):
            eparts[j, p] = edge[piece * j : piece * (j + 1)]

    c10 = exchange(10, "y", lambda j: eparts.at[j], lambda d: ers.at[d])
    arrive(c10)
    if stop <= 10:
        return finish()
    total = eparts[y].astype(f32)
    for d in range(1, ny):
        total += ers[d].astype(f32)
    e1[...] = total.astype(bf16)
    c11 = exchange(11, "a", lambda j: e1, lambda d: eex.at[d])
    arrive(c11)
    if stop <= 11:
        return finish()
    for d in range(1, na):
        total += eex[d].astype(f32)
    fin[y] = total.astype(bf16)
    c12 = exchange(12, "y", lambda j: fin.at[y], lambda d: fin.at[y])
    arrive(c12)
    if stop <= 12:
        return finish()
    for j in range(ny):
        for p in range(2):
            out_ref[p, piece * j : piece * (j + 1), :] = fin[j, p].astype(f32)

    finish()


def body(nz, ny, nx, nh, stop, cid, grads, positions, raw, out_proj, value_proj, decoders, ids, act):
    f32, bf16 = jnp.float32, jnp.bfloat16
    out_proj, value_proj, ids, act = out_proj.T, value_proj.T, ids.T, act.T
    w = grads.shape[1]
    listed, tokens = ids.shape
    feats, width = decoders.shape
    na, rows, piece = nz * nx, nh * 16, 2 * listed // ny
    wx = nx * w
    lanes_w = -(-w // 128) * 128
    lanes_x = -(-wx // 128) * 128
    tall_w = -(-w // 16) * 16
    vmem = pltpu.VMEM
    scratch = [
        vmem(raw.shape, f32),
        vmem(out_proj.shape, bf16),
        vmem((nz,) + value_proj.shape, bf16),
        vmem(ids.shape, jnp.int32),
        vmem(act.shape, f32),
        vmem((feats, width), bf16),
        vmem((nh, 8, lanes_w), f32),
        vmem((na, 8, lanes_w), f32),
        vmem((ny, nz, 8, lanes_x), f32),
        vmem((8, width), f32),
        vmem((nh, 16, tokens), f32),
        vmem((nh, 16, tokens), f32),
        vmem((ny, 8, 2 * HD), f32),
        vmem((ny, 8, 2 * HD), f32),
        vmem((na, 8, 2 * HD), f32),
        vmem((ny, 8, 2 * HD), f32),
        vmem((nh, nz, 16, lanes_w), bf16),
        vmem((nh, nz, 16, lanes_w), bf16),
        vmem((nx, tall_w, rows), bf16),
        vmem((nx, ny, tall_w, rows), bf16),
        vmem((nz, ny, wx, rows), bf16),
        vmem((ny, 2, piece, tokens), bf16),
        vmem((ny, 2, piece, tokens), bf16),
        vmem((2, piece, tokens), bf16),
        vmem((na, 2, piece, tokens), bf16),
        vmem((ny, 2, piece, tokens), bf16),
        vmem((2, tokens, rows), bf16),
        vmem((tokens, 2 * listed), jnp.int32),
        pltpu.SemaphoreType.DMA((6,)),
        pltpu.SemaphoreType.DMA((13, 8)),
        pltpu.SemaphoreType.DMA((13, 8)),
        pltpu.SemaphoreType.DMA((48,)),
        pltpu.SemaphoreType.DMA((48,)),
    ]
    in_vmem = pl.BlockSpec(memory_space=pltpu.VMEM)
    edges = pl.pallas_call(
        functools.partial(kernel, nz, ny, nx, nh, stop),
        out_shape=jax.ShapeDtypeStruct((2, 2 * listed, tokens), f32),
        in_specs=[pl.BlockSpec(memory_space=pltpu.SMEM), in_vmem]
        + [pl.BlockSpec(memory_space=pl.ANY)] * 6,
        out_specs=in_vmem,
        scratch_shapes=scratch,
        compiler_params=pltpu.CompilerParams(
            collective_id=cid, has_side_effects=True, vmem_limit_bytes=60 * 1024 * 1024
        ),
    )(positions, grads, raw, out_proj, value_proj, decoders, ids, act)
    return edges.reshape(4, listed, tokens).transpose(0, 2, 1)


def solution(mesh, sizes=(NZ, NY, NX, NH), stop=99, cid=0):
    placed = (
        P("head", "feat"),
        P(),
        P("head", None, None),
        P("head", "feat"),
        P("head", "feat"),
        P("feat", None),
        P(),
        P(),
    )
    return jax.shard_map(
        functools.partial(body, *sizes, stop, cid),
        mesh=mesh,
        in_specs=placed,
        out_specs=P("head", None, None),
        check_vma=False,
    )
```

time: 97.9 us -> 85.1 us (0.87)
  the two profiles are of different devices: /device:TPU:8 before, /device:TPU:2 now
where the time goes in v2:
time: 85.1 us; the launch traced here: 85 us
  Pallas kernels  83.3 us (98%)
  local copies, waits for them, and re-layouts  1.67 us (2%)
    pallas_call x1, Pallas kernels, body(): pl.pallas_call(functools.partial(kernel, nz, ny, nx, nh, stop), out_shape...  83.3 us

profile of v2, /device:TPU:2, one launch (start us, length us, event | category | flops | bytes accessed | tf_op | source)
XLA Modules:
  0.0 85.0 jit_solution(2971779719448337658)
XLA Ops:
  0.0 83.3 %shard_map.82 = f32[2,128,256]{2,1,0:T(8,128)} custom-call(s32[32]{0:T(128)} %pos_ref.1, bf16[4,84]{1,0:T(4,128)(2,1)} %grads_ref.1, f32[4,32,256]{2,1,0:T(8,128)} %raw_hbm.1, bf16[84,512]{1,0:T(8,128)(2,1)} %bitcast.8, bf16[84,512]{1,0:T(8,128)(2,1)} %bitcast.9, bf16[384,5376]{1,0:T(8,128)(2,1)} %dec_hbm.1, s32[64,256]{1,0:T(8,128)} %bitcast.10, ...), custom_call_target="tpu_custom_call" | custom-call | tf_op jit(solution)/shard_map/pallas_call | solution.py:423
  83.3 1.7 %copy.10 = f32[4,256,64]{1,2,0:T(8,128)} copy(f32[4,256,64]{1,2,0:T(8,128)} %bitcast.7) | data formatting | bytes 524288

commit v3 on v2

--- a/solution.py
+++ b/solution.py
@@ -39,40 +39,39 @@
     z = lax.div(f, nx * ny)
     a = z * nx + x
 
-    def head_at(d):
-        j = lax.rem(g + d, nh)
-        return j, (f, j)
-
-    def y_at(d):
-        j = lax.rem(y + d, ny)
-        return j, (z * (nx * ny) + j * nx + x, g)
-
-    def a_at(d):
-        j = lax.rem(a + d, na)
-        return j, (lax.div(j, nx) * (nx * ny) + y * nx + lax.rem(j, nx), g)
-
-    def x_at(d):
-        j = lax.rem(x + d, nx)
-        return j, (f - x + j, g)
-
-    def z_at(d):
-        j = lax.rem(z + d, nz)
-        return j, (f + (j - z) * (nx * ny), g)
-
-    groups = {"h": (head_at, nh), "y": (y_at, ny), "a": (a_at, na), "x": (x_at, nx)}
+    def place(dz, dy, dx, dh):
+        zj, yj, xj = lax.rem(z + dz, nz), lax.rem(y + dy, ny), lax.rem(x + dx, nx)
+        gj = lax.rem(g + dh, nh)
+        return zj, yj, xj, gj, (zj * (nx * ny) + yj * nx + xj, gj)
+
+    def far_first(n):
+        return sorted(range(1, n), key=lambda d: -min(d, n - d))
+
+    groups = {
+        "h": [(d, place(0, 0, 0, d)) for d in far_first(nh)],
+        "y": [(d, place(0, d, 0, 0)) for d in far_first(ny)],
+        "x": [(d, place(0, 0, d, 0)) for d in far_first(nx)],
+        "a": [(nx * k + d, place(k, 0, d, 0)) for k in range(1, nz) for d in far_first(nx) + [0]]
+        + [(d, place(0, 0, d, 0)) for d in far_first(nx)],
+        "zh": [(nh * k + d, place(k, 0, 0, d)) for k in range(1, nz) for d in [0, 1, nh - 1]]
+        + [(d, place(0, 0, 0, d)) for d in far_first(nh)]
+        + [(nh * k + d, place(k, 0, 0, d)) for k in range(1, nz) for d in range(2, nh - 1)],
+    }
+    if nh == 2:
+        groups["zh"] = [(2, place(1, 0, 0, 0)), (3, place(1, 0, 0, 1)), (1, place(0, 0, 0, 1))]
 
     barrier = pltpu.get_barrier_semaphore()
-    for name in ("h", "y", "a"):
-        at, n = groups[name]
-        for d in range(1, n):
-            pl.semaphore_signal(barrier, inc=1, device_id=at(d)[1], device_id_type=MESH)
+    greet = groups["a"] + groups["y"] + groups["zh"]
+    greet = [who for slot, who in greet if not (who is groups["zh"][0][1])]
+    for who in greet:
+        pl.semaphore_signal(barrier, inc=1, device_id=who[4], device_id_type=MESH)
 
     loads = {}
     for i, (name, src, dst) in enumerate(
         (
             ("raw", raw_hbm, raw_ref),
             ("outp", outp_hbm, outp_ref),
-            ("valp", valp_hbm, valp_ref.at[z]),
+            ("valp", valp_hbm, valp_ref),
             ("ids", ids_hbm, ids_ref),
             ("act", act_hbm, act_ref),
             ("dec", dec_hbm, dec),
@@ -86,21 +85,18 @@
         loaded.append(name)
 
     def exchange(stage, group, src, dst):
-        at, n = groups[group]
-        copies = []
-        for d in range(1, n):
-            j, device = at(d)
-            copy = pltpu.make_async_remote_copy(
-                src_ref=src(j),
-                dst_ref=dst(d),
-                send_sem=ssem.at[stage, d],
-                recv_sem=rsem.at[stage, d],
-                device_id=device,
+        copies = {}
+        for slot, who in groups[group]:
+            copies[slot] = pltpu.make_async_remote_copy(
+                src_ref=src(who),
+                dst_ref=dst(slot),
+                send_sem=ssem.at[stage, slot],
+                recv_sem=rsem.at[stage, slot],
+                device_id=who[4],
                 device_id_type=MESH,
             )
-            copy.start()
-            copies.append(copy)
-            started.append(copy)
+            copies[slot].start()
+            started.append(copies[slot])
         return copies
 
     def send(slot, src, dst, device):
@@ -117,7 +113,7 @@
         return copy
 
     def arrive(copies):
-        for copy in copies:
+        for copy in copies.values() if isinstance(copies, dict) else copies:
             copy.wait_recv()
             arrived.append(copy)
 
@@ -139,16 +135,15 @@
     gall[g, :, 0:w] = mine
     ga[a] = zero_lanes
     ga[a, :, 0:w] = mine
-    pl.semaphore_wait(barrier, nh - 1 + ny - 1 + na - 1)
+    pl.semaphore_wait(barrier, len(greet))
     c0 = exchange(0, "h", lambda j: gall.at[g], lambda d: gall.at[g])
-    load("valp")
-    cv = send(0, valp_ref.at[z], valp_ref.at[z], z_at(1)[1])
 
     load("raw")
     for j in range(nh):
         for h in range(4):
             psend[j, 4 * h : 4 * h + 4, :] = raw_ref[h, 4 * j : 4 * j + 4, :]
     tsend[...] = jnp.zeros_like(tsend)
+    gfull[...] = jnp.zeros_like(gfull)
     load("outp")
 
     arrive(c0)
@@ -160,9 +155,7 @@
     partial = dot(jnp.where(low, both, 0.0).astype(bf16), outp_ref[:, 0:half])
     partial += dot(jnp.where(low, 0.0, both).astype(bf16), outp_ref[:, half : 2 * half])
     part[...] = partial.reshape(ny, 8, half)
-    c4 = exchange(4, "y", lambda j: part.at[j], lambda d: rs.at[d])
-    c1 = exchange(1, "h", lambda j: psend.at[j], lambda d: pall.at[g])
-    pall[g] = psend[g]
+    c4 = exchange(4, "y", lambda who: part.at[who[1]], lambda d: rs.at[d])
     c2 = exchange(2, "a", lambda j: ga.at[a], lambda d: ga.at[a])
 
     arrive(c4)
@@ -177,7 +170,8 @@
     arrive(c2)
     for k in range(nz):
         for i in range(nx):
-            gy[y, k, :, w * i : w * i + w] = ga[k * nx + i, :, 0:w]
+            gy[y, 4 * k : 4 * k + 4, w * i : w * i + w] = ga[k * nx + i, 0:4, 0:w]
+    c3 = exchange(3, "y", lambda j: gy.at[y], lambda d: gy.at[y])
 
     r = lax.broadcasted_iota(jnp.int32, (rows, ny * 8), 0)
     c = lax.broadcasted_iota(jnp.int32, (rows, ny * 8), 1)
@@ -196,24 +190,6 @@
     hall[y] = total.astype(bf16).astype(f32)
     c6 = exchange(6, "y", lambda j: hall.at[y], lambda d: hall.at[y])
 
-    arrive(c1)
-    raw = pall[...].reshape(rows, tokens)
-    row_t = lax.rem(lax.broadcasted_iota(jnp.int32, raw.shape, 0), 4)
-    spot = lax.broadcasted_iota(jnp.int32, raw.shape, 1)
-    row_pos = jnp.zeros(raw.shape, jnp.int32)
-    own_pos = []
-    for t in range(4):
-        own_pos.append(pos_ref[4 * g + t])
-        row_pos = jnp.where(row_t == t, own_pos[t], row_pos)
-    masked = jnp.where(spot <= row_pos, raw, 0.0)
-    pattern = masked / jnp.sum(masked, axis=1, keepdims=True)
-    pat = pattern.T
-    pat_hi = pat.astype(bf16)
-    pat_lo = (pat - pat_hi.astype(f32)).astype(bf16)
-    pats[0] = pat_hi
-    pats[1] = pat_lo
-
-    arrive([cv])
     arrive(c6)
     if stop <= 6:
         return finish()
@@ -221,13 +197,12 @@
     spread = dot(choose, hin)
     first = jnp.where(fits & ~upper, spread, 0.0).astype(bf16)
     second = jnp.where(fits & upper, spread, 0.0).astype(bf16)
-    for k in range(nz):
-        through = dot(first, valp_ref[k, :, 0:half], NT)
-        through += dot(second, valp_ref[k, :, half : 2 * half], NT)
-        tsend[:, k, :, 0:w] = through.astype(bf16).reshape(nh, 16, w)
-    c7 = exchange(7, "h", lambda j: tsend.at[j], lambda d: tall.at[g])
-    tall[g] = tsend[g]
-    c3 = exchange(3, "y", lambda j: gy.at[y], lambda d: gy.at[y])
+    load("valp")
+    through = dot(first, valp_ref[:, 0:half], NT)
+    through += dot(second, valp_ref[:, half : 2 * half], NT)
+    tsend[:, :, 0:w] = through.astype(bf16).reshape(nh, 16, w)
+    c7 = exchange(7, "zh", lambda who: tsend.at[who[3]], lambda d: tall.at[z, g])
+    tall[z, g] = tsend[g]
 
     load("ids")
     load("act")
@@ -240,15 +215,20 @@
     tall_w = ax.shape[1]
 
     def turned(k):
-        block = tall[:, k].reshape(rows, tall.shape[3]).astype(f32).T
+        block = tall[k].reshape(rows, tall.shape[3]).astype(f32).T
         return block[0:tall_w].astype(bf16)
 
     ax[x] = turned(0)
     cx = exchange(8, "x", lambda j: ax.at[x], lambda d: ax.at[x])
     bx[x, 0] = turned(1)
     cy = exchange(9, "y", lambda j: bx.at[x, 0], lambda d: bx.at[x, d])
-    right, left = x_at(1)[1], x_at(nx - 1)[1]
-    from_left, from_right = x_at(nx - 1)[0], x_at(1)[0]
+    right, left = place(0, 0, 1, 0)[4], place(0, 0, nx - 1, 0)[4]
+    from_left, from_right = lax.rem(x + nx - 1, nx), lax.rem(x + 1, nx)
+
+    def y_at(d):
+        who = place(0, d, 0, 0)
+        return who[1], who[4]
+
     hops = {}
 
     def pass_on(d):
@@ -266,15 +246,17 @@
         far[d] = send(1 + i, mine_y, mine_y, y_at(d)[1])
     order = (1, ny - 1, 2, ny - 2, 3, ny - 3, 4) if ny == 8 else (1,)
     for d in order:
-        arrive([cy[d - 1]])
+        arrive([cy[d]])
         pass_on(d)
+    c1 = exchange(1, "h", lambda who: psend.at[who[3]], lambda d: pall.at[g])
+    pall[g] = psend[g]
 
     load("dec")
     arrive(c3)
     for k in range(nz):
         for j in range(ny):
             at = wx * (k * ny + j)
-            gfull[:, at : at + wx] = gy[j, k, :, 0:wx]
+            gfull[0:4, at : at + wx] = gy[j, 4 * k : 4 * k + 4, 0:wx]
 
     cut = (wx // 32) * 16
     if ny == 8:
@@ -295,6 +277,23 @@
         arrive([hops["l", d]])
         if d > ny // 2 - 1:
             hops["l2", d] = send(40 + d, bx.at[from_right, d], bx.at[from_right, d], left)
+
+    arrive(c1)
+    raw = pall[...].reshape(rows, tokens)
+    row_t = lax.rem(lax.broadcasted_iota(jnp.int32, raw.shape, 0), 4)
+    spot = lax.broadcasted_iota(jnp.int32, raw.shape, 1)
+    row_pos = jnp.zeros(raw.shape, jnp.int32)
+    own_pos = []
+    for t in range(4):
+        own_pos.append(pos_ref[4 * g + t])
+        row_pos = jnp.where(row_t == t, own_pos[t], row_pos)
+    masked = jnp.where(spot <= row_pos, raw, 0.0)
+    pattern = masked / jnp.sum(masked, axis=1, keepdims=True)
+    pat = pattern.T
+    pat_hi = pat.astype(bf16)
+    pat_lo = (pat - pat_hi.astype(f32)).astype(bf16)
+    pats[0] = pat_hi
+    pats[1] = pat_lo
 
     straight = dot(gfull[...].astype(bf16), dec[...], NT)
 
@@ -346,7 +345,7 @@
         for j in range(ny):
             eparts[j, p] = edge[piece * j : piece * (j + 1)]
 
-    c10 = exchange(10, "y", lambda j: eparts.at[j], lambda d: ers.at[d])
+    c10 = exchange(10, "y", lambda who: eparts.at[who[1]], lambda d: ers.at[d])
     arrive(c10)
     if stop <= 10:
         return finish()
@@ -367,7 +366,7 @@
         return finish()
     for j in range(ny):
         for p in range(2):
-            out_ref[p, piece * j : piece * (j + 1), :] = fin[j, p].astype(f32)
+            out_ref[p, piece * j : piece * (j + 1), :] = fin[j, p]
 
     finish()
 
@@ -387,13 +386,13 @@
     scratch = [
         vmem(raw.shape, f32),
         vmem(out_proj.shape, bf16),
-        vmem((nz,) + value_proj.shape, bf16),
+        vmem(value_proj.shape, bf16),
         vmem(ids.shape, jnp.int32),
         vmem(act.shape, f32),
         vmem((feats, width), bf16),
         vmem((nh, 8, lanes_w), f32),
         vmem((na, 8, lanes_w), f32),
-        vmem((ny, nz, 8, lanes_x), f32),
+        vmem((ny, 8, lanes_x), f32),
         vmem((8, width), f32),
         vmem((nh, 16, tokens), f32),
         vmem((nh, 16, tokens), f32),
@@ -401,8 +400,8 @@
         vmem((ny, 8, 2 * HD), f32),
         vmem((na, 8, 2 * HD), f32),
         vmem((ny, 8, 2 * HD), f32),
-        vmem((nh, nz, 16, lanes_w), bf16),
-        vmem((nh, nz, 16, lanes_w), bf16),
+        vmem((nh, 16, lanes_w), bf16),
+        vmem((nz, nh, 16, lanes_w), bf16),
         vmem((nx, tall_w, rows), bf16),
         vmem((nx, ny, tall_w, rows), bf16),
         vmem((nz, ny, wx, rows), bf16),
@@ -414,15 +413,15 @@
         vmem((2, tokens, rows), bf16),
         vmem((tokens, 2 * listed), jnp.int32),
         pltpu.SemaphoreType.DMA((6,)),
-        pltpu.SemaphoreType.DMA((13, 8)),
-        pltpu.SemaphoreType.DMA((13, 8)),
+        pltpu.SemaphoreType.DMA((13, 16)),
+        pltpu.SemaphoreType.DMA((13, 16)),
         pltpu.SemaphoreType.DMA((48,)),
         pltpu.SemaphoreType.DMA((48,)),
     ]
     in_vmem = pl.BlockSpec(memory_space=pltpu.VMEM)
     edges = pl.pallas_call(
         functools.partial(kernel, nz, ny, nx, nh, stop),
-        out_shape=jax.ShapeDtypeStruct((2, 2 * listed, tokens), f32),
+        out_shape=jax.ShapeDtypeStruct((2, 2 * listed, tokens), bf16),
         in_specs=[pl.BlockSpec(memory_space=pltpu.SMEM), in_vmem]
         + [pl.BlockSpec(memory_space=pl.ANY)] * 6,
         out_specs=in_vmem,
@@ -431,7 +430,7 @@
             collective_id=cid, has_side_effects=True, vmem_limit_bytes=60 * 1024 * 1024
         ),
     )(positions, grads, raw, out_proj, value_proj, decoders, ids, act)
-    return edges.reshape(4, listed, tokens).transpose(0, 2, 1)
+    return edges.astype(f32).reshape(4, listed, tokens).transpose(0, 2, 1)
 
 
 def solution(mesh, sizes=(NZ, NY, NX, NH), stop=99, cid=0):

time: 85.1 us -> 81.5 us (0.958)
  the two profiles are of different devices: /device:TPU:2 before, /device:TPU:8 now
where the time goes in v3:
time: 81.5 us; the launch traced here: 81.3 us
  Pallas kernels  79.7 us (98%)
  other arithmetic  1.63 us (2%)
    pallas_call x1, Pallas kernels, body(): pl.pallas_call(functools.partial(kernel, nz, ny, nx, nh, stop), out_shape...  79.7 us

profile of v3, /device:TPU:8, one launch (start us, length us, event | category | flops | bytes accessed | tf_op | source)
XLA Modules:
  0.0 81.3 jit_solution(13081532786527685939)
XLA Ops:
  0.0 79.7 %shard_map.82 = bf16[2,128,256]{2,1,0:T(8,128)(2,1)} custom-call(s32[32]{0:T(128)} %pos_ref.1, bf16[4,84]{1,0:T(4,128)(2,1)} %grads_ref.1, f32[4,32,256]{2,1,0:T(8,128)} %raw_hbm.1, bf16[84,512]{1,0:T(8,128)(2,1)} %bitcast.9, bf16[84,512]{1,0:T(8,128)(2,1)} %bitcast.10, bf16[384,5376]{1,0:T(8,128)(2,1)} %dec_hbm.1, s32[64,256]{1,0:T(8,128)} %bitcast.11, ...), custom_call_target="tpu_custom_call" | custom-call | tf_op jit(solution)/shard_map/pallas_call | solution.py:422
  79.7 1.6 %convert_bitcast_fusion = f32[4,256,64]{1,2,0:T(8,128)} fusion(bf16[4,64,256]{2,1,0:T(8,128)(2,1)} %bitcast.8), kind=kLoop, calls=%fused_computation | loop fusion | flops 65536 | bytes 393216 | tf_op jit(solution)/shard_map/transpose | solution.py:433

commit v4 on v3

--- a/solution.py
+++ b/solution.py
@@ -23,7 +23,7 @@
     out_ref,
     raw_ref, outp_ref, valp_ref, ids_ref, act_ref, dec, gall, ga, gy, gfull, pall, psend, part, rs, ex, hall, tsend, tall, ax, bx, thr,
     eparts, ers, e1, eex, fin, pats, ids_t,
-    in_sem, ssem, rsem, side_s, side_r,
+    in_sem, ssem, rsem,
 ):
     f32, bf16 = jnp.float32, jnp.bfloat16
     na = nz * nx
@@ -53,16 +53,12 @@
         "x": [(d, place(0, 0, d, 0)) for d in far_first(nx)],
         "a": [(nx * k + d, place(k, 0, d, 0)) for k in range(1, nz) for d in far_first(nx) + [0]]
         + [(d, place(0, 0, d, 0)) for d in far_first(nx)],
-        "zh": [(nh * k + d, place(k, 0, 0, d)) for k in range(1, nz) for d in [0, 1, nh - 1]]
-        + [(d, place(0, 0, 0, d)) for d in far_first(nh)]
-        + [(nh * k + d, place(k, 0, 0, d)) for k in range(1, nz) for d in range(2, nh - 1)],
+        "zh": [(d, place(1, 0, 0, d)) for d in [0] + far_first(nh)[::-1]],
     }
-    if nh == 2:
-        groups["zh"] = [(2, place(1, 0, 0, 0)), (3, place(1, 0, 0, 1)), (1, place(0, 0, 0, 1))]
 
     barrier = pltpu.get_barrier_semaphore()
-    greet = groups["a"] + groups["y"] + groups["zh"]
-    greet = [who for slot, who in greet if not (who is groups["zh"][0][1])]
+    greet = groups["a"] + groups["y"] + groups["zh"][1:] + groups["h"]
+    greet = [who for slot, who in greet]
     for who in greet:
         pl.semaphore_signal(barrier, inc=1, device_id=who[4], device_id_type=MESH)
 
@@ -84,49 +80,54 @@
         loads[name].wait()
         loaded.append(name)
 
-    def exchange(stage, group, src, dst):
+    def exchange(stage, group, src, dst, whole, each=None):
         copies = {}
         for slot, who in groups[group]:
             copies[slot] = pltpu.make_async_remote_copy(
                 src_ref=src(who),
                 dst_ref=dst(slot),
-                send_sem=ssem.at[stage, slot],
-                recv_sem=rsem.at[stage, slot],
+                send_sem=ssem.at[stage],
+                recv_sem=rsem.at[stage if each is None else each + slot],
                 device_id=who[4],
                 device_id_type=MESH,
             )
             copies[slot].start()
-            started.append(copies[slot])
-        return copies
-
-    def send(slot, src, dst, device):
+        sent.append((stage, whole))
+        return copies if each is not None else (stage, whole)
+
+    def send(sems, src, dst, device):
         copy = pltpu.make_async_remote_copy(
             src_ref=src,
             dst_ref=dst,
-            send_sem=side_s.at[slot],
-            recv_sem=side_r.at[slot],
+            send_sem=ssem.at[sems[0]],
+            recv_sem=rsem.at[sems[1]],
             device_id=device,
             device_id_type=MESH,
         )
         copy.start()
-        started.append(copy)
         return copy
 
-    def arrive(copies):
-        for copy in copies.values() if isinstance(copies, dict) else copies:
-            copy.wait_recv()
-            arrived.append(copy)
+    def all_of(stage, whole):
+        return pltpu.make_async_remote_copy(
+            src_ref=whole,
+            dst_ref=whole,
+            send_sem=ssem.at[stage],
+            recv_sem=rsem.at[stage],
+            device_id=groups["h"][0][1][4],
+            device_id_type=MESH,
+        )
+
+    def arrive(one):
+        all_of(*one).wait_recv()
 
     def finish():
-        for copy in started:
-            if not any(copy is other for other in arrived):
-                copy.wait_recv()
-            copy.wait_send()
+        for one in sent:
+            all_of(*one).wait_send()
         for name, copy in loads.items():
             if name not in loaded:
                 copy.wait()
 
-    started, arrived, loaded = [], [], []
+    sent, loaded = [], []
 
     own = grads_ref[...].astype(f32)
     mine = jnp.concatenate([own, own], axis=0)
@@ -136,7 +137,7 @@
     ga[a] = zero_lanes
     ga[a, :, 0:w] = mine
     pl.semaphore_wait(barrier, len(greet))
-    c0 = exchange(0, "h", lambda j: gall.at[g], lambda d: gall.at[g])
+    c0 = exchange(0, "h", lambda j: gall.at[g], lambda d: gall.at[g], gall.at[0 : nh - 1])
 
     load("raw")
     for j in range(nh):
@@ -155,8 +156,8 @@
     partial = dot(jnp.where(low, both, 0.0).astype(bf16), outp_ref[:, 0:half])
     partial += dot(jnp.where(low, 0.0, both).astype(bf16), outp_ref[:, half : 2 * half])
     part[...] = partial.reshape(ny, 8, half)
-    c4 = exchange(4, "y", lambda who: part.at[who[1]], lambda d: rs.at[d])
-    c2 = exchange(2, "a", lambda j: ga.at[a], lambda d: ga.at[a])
+    c4 = exchange(4, "y", lambda who: part.at[who[1]], lambda d: rs.at[d], rs.at[0 : ny - 1])
+    c2 = exchange(2, "a", lambda j: ga.at[a], lambda d: ga.at[a], ga.at[0 : na - 1])
 
     arrive(c4)
     if stop <= 4:
@@ -165,13 +166,13 @@
     for d in range(1, ny):
         total += rs[d]
     ex[0] = total
-    c5 = exchange(5, "a", lambda j: ex.at[0], lambda d: ex.at[d])
+    c5 = exchange(5, "a", lambda j: ex.at[0], lambda d: ex.at[d], ex.at[0 : na - 1])
 
     arrive(c2)
     for k in range(nz):
         for i in range(nx):
             gy[y, 4 * k : 4 * k + 4, w * i : w * i + w] = ga[k * nx + i, 0:4, 0:w]
-    c3 = exchange(3, "y", lambda j: gy.at[y], lambda d: gy.at[y])
+    c3 = exchange(3, "y", lambda j: gy.at[y], lambda d: gy.at[y], gy.at[0 : ny - 1])
 
     r = lax.broadcasted_iota(jnp.int32, (rows, ny * 8), 0)
     c = lax.broadcasted_iota(jnp.int32, (rows, ny * 8), 1)
@@ -188,7 +189,7 @@
     for d in range(1, na):
         total += ex[d]
     hall[y] = total.astype(bf16).astype(f32)
-    c6 = exchange(6, "y", lambda j: hall.at[y], lambda d: hall.at[y])
+    c6 = exchange(6, "y", lambda j: hall.at[y], lambda d: hall.at[y], hall.at[0 : ny - 1])
 
     arrive(c6)
     if stop <= 6:
@@ -201,7 +202,10 @@
     through = dot(first, valp_ref[:, 0:half], NT)
     through += dot(second, valp_ref[:, half : 2 * half], NT)
     tsend[:, :, 0:w] = through.astype(bf16).reshape(nh, 16, w)
-    c7 = exchange(7, "zh", lambda who: tsend.at[who[3]], lambda d: tall.at[z, g])
+    c7 = exchange(7, "zh", lambda who: tsend.at[who[3]], lambda d: tall.at[z, g], tall.at[0])
+    c13 = exchange(
+        13, "h", lambda who: tsend.at[who[3]], lambda d: tall.at[z, g], tall.at[0, 0 : nh - 1]
+    )
     tall[z, g] = tsend[g]
 
     load("ids")
@@ -209,6 +213,7 @@
     ids = ids_ref[...] - f * feats
     ids_t[...] = jnp.concatenate([ids, ids], axis=0).T
 
+    arrive(c13)
     arrive(c7)
     if stop <= 7:
         return finish()
@@ -219,9 +224,9 @@
         return block[0:tall_w].astype(bf16)
 
     ax[x] = turned(0)
-    cx = exchange(8, "x", lambda j: ax.at[x], lambda d: ax.at[x])
+    cx = exchange(8, "x", lambda j: ax.at[x], lambda d: ax.at[x], ax.at[0 : nx - 1])
     bx[x, 0] = turned(1)
-    cy = exchange(9, "y", lambda j: bx.at[x, 0], lambda d: bx.at[x, d])
+    cy = exchange(9, "y", lambda j: bx.at[x, 0], lambda d: bx.at[x, d], bx.at[0, 0 : ny - 1], 24)
     right, left = place(0, 0, 1, 0)[4], place(0, 0, nx - 1, 0)[4]
     from_left, from_right = lax.rem(x + nx - 1, nx), lax.rem(x + 1, nx)
 
@@ -230,10 +235,13 @@
         return who[1], who[4]
 
     hops = {}
+    reach = ny // 2
 
     def pass_on(d):
-        hops["r", d] = send(20 + 2 * d, bx.at[x, d], bx.at[x, d], right)
-        hops["l", d] = send(21 + 2 * d, bx.at[x, d], bx.at[x, d], left)
+        sems = (14, 32 + d if d < reach else 14)
+        hops["r", d] = send(sems, bx.at[x, d], bx.at[x, d], right)
+        sems = (15, 32 + d if d >= reach else 15)
+        hops["l", d] = send(sems, bx.at[x, d], bx.at[x, d], left)
 
     pass_on(0)
     arrive(cx)
@@ -243,12 +251,12 @@
     far = {}
     steps = (2, ny - 2, 1, ny - 1) if ny == 8 else (1,)
     for i, d in enumerate(steps):
-        far[d] = send(1 + i, mine_y, mine_y, y_at(d)[1])
+        far[d] = send((18, 19 + i if i < 2 and ny == 8 else 18), mine_y, mine_y, y_at(d)[1])
     order = (1, ny - 1, 2, ny - 2, 3, ny - 3, 4) if ny == 8 else (1,)
     for d in order:
-        arrive([cy[d]])
+        cy[d].wait_recv()
         pass_on(d)
-    c1 = exchange(1, "h", lambda who: psend.at[who[3]], lambda d: pall.at[g])
+    c1 = exchange(1, "h", lambda who: psend.at[who[3]], lambda d: pall.at[g], pall.at[0 : nh - 1])
     pall[g] = psend[g]
 
     load("dec")
@@ -260,23 +268,23 @@
 
     cut = (wx // 32) * 16
     if ny == 8:
-        arrive([far[2]])
+        far[2].wait_recv()
         back = thr.at[0, y_at(ny - 2)[0]]
-        far[3] = send(5, back, back, y_at(1)[1])
+        far[3] = send((18, 18), back, back, y_at(1)[1])
         back = thr.at[0, y_at(ny - 2)[0], 0:cut]
-        far["low"] = send(6, back, back, y_at(2)[1])
-        arrive([far[ny - 2]])
+        far["low"] = send((18, 18), back, back, y_at(2)[1])
+        far[ny - 2].wait_recv()
         back = thr.at[0, y_at(2)[0]]
-        far[ny - 3] = send(7, back, back, y_at(ny - 1)[1])
+        far[ny - 3] = send((18, 18), back, back, y_at(ny - 1)[1])
         back = thr.at[0, y_at(2)[0], cut:wx]
-        far["high"] = send(8, back, back, y_at(ny - 2)[1])
+        far["high"] = send((18, 18), back, back, y_at(ny - 2)[1])
     for d in (0,) + order:
-        arrive([hops["r", d]])
-        if d <= ny // 2 - 1:
-            hops["r2", d] = send(40 + d, bx.at[from_left, d], bx.at[from_left, d], right)
-        arrive([hops["l", d]])
-        if d > ny // 2 - 1:
-            hops["l2", d] = send(40 + d, bx.at[from_right, d], bx.at[from_right, d], left)
+        if d < reach:
+            hops["r", d].wait_recv()
+            send((16, 16), bx.at[from_left, d], bx.at[from_left, d], right)
+        else:
+            hops["l", d].wait_recv()
+            send((16, 17), bx.at[from_right, d], bx.at[from_right, d], left)
 
     arrive(c1)
     raw = pall[...].reshape(rows, tokens)
@@ -297,18 +305,21 @@
 
     straight = dot(gfull[...].astype(bf16), dec[...], NT)
 
-    for d in far:
-        if not any(far[d] is other for other in arrived):
-            arrive([far[d]])
+    sent.append((18, thr.at[0, 0 : ny - 1]))
+    arrive((18, thr.at[0, 0 : ny - 3] if ny == 8 else thr.at[0, 0 : ny - 1]))
     span = ny * wx
     scores = dot(dec[:, 0:span], thr[0].reshape(span, rows))
-    for d in range(ny):
-        arrive([hops["r2" if d <= ny // 2 - 1 else "l2", d]])
+    sent.extend([(14, bx.at[0]), (15, bx.at[0]), (16, bx.at[0])])
+    arrive((14, bx.at[0, 0 : ny - reach]))
+    arrive((15, bx.at[0, 0:reach]))
+    for lane_way, first_d, last_d in ((16, 0, reach), (17, reach, ny)):
+        arrive((lane_way, bx.at[0, first_d:last_d]))
+        if stop > 9:
+            for d in range(first_d, last_d):
+                joined = [bx[i, d].astype(f32)[0:w] for i in range(nx)]
+                thr[1, y_at(ny - d)[0]] = jnp.concatenate(joined, axis=0).astype(bf16)
     if stop <= 9:
         return finish()
-    for d in range(ny):
-        joined = [bx[i, d].astype(f32)[0:w] for i in range(nx)]
-        thr[1, y_at(ny - d)[0]] = jnp.concatenate(joined, axis=0).astype(bf16)
     scores += dot(dec[:, span : 2 * span], thr[1].reshape(span, rows))
     sc_hi = scores.astype(bf16)
     sc_lo = (scores - sc_hi.astype(f32)).astype(bf16)
@@ -345,7 +356,7 @@
         for j in range(ny):
             eparts[j, p] = edge[piece * j : piece * (j + 1)]
 
-    c10 = exchange(10, "y", lambda who: eparts.at[who[1]], lambda d: ers.at[d])
+    c10 = exchange(10, "y", lambda who: eparts.at[who[1]], lambda d: ers.at[d], ers.at[0 : ny - 1])
     arrive(c10)
     if stop <= 10:
         return finish()
@@ -353,14 +364,14 @@
     for d in range(1, ny):
         total += ers[d].astype(f32)
     e1[...] = total.astype(bf16)
-    c11 = exchange(11, "a", lambda j: e1, lambda d: eex.at[d])
+    c11 = exchange(11, "a", lambda j: e1, lambda d: eex.at[d], eex.at[0 : na - 1])
     arrive(c11)
     if stop <= 11:
         return finish()
     for d in range(1, na):
         total += eex[d].astype(f32)
     fin[y] = total.astype(bf16)
-    c12 = exchange(12, "y", lambda j: fin.at[y], lambda d: fin.at[y])
+    c12 = exchange(12, "y", lambda j: fin.at[y], lambda d: fin.at[y], fin.at[0 : ny - 1])
     arrive(c12)
     if stop <= 12:
         return finish()
@@ -413,10 +424,8 @@
         vmem((2, tokens, rows), bf16),
         vmem((tokens, 2 * listed), jnp.int32),
         pltpu.SemaphoreType.DMA((6,)),
-        pltpu.SemaphoreType.DMA((13, 16)),
-        pltpu.SemaphoreType.DMA((13, 16)),
-        pltpu.SemaphoreType.DMA((48,)),
-        pltpu.SemaphoreType.DMA((48,)),
+        pltpu.SemaphoreType.DMA((19,)),
+        pltpu.SemaphoreType.DMA((32 + ny,)),
     ]
     in_vmem = pl.BlockSpec(memory_space=pltpu.VMEM)
     edges = pl.pallas_call(

time: 81.5 us -> 78 us (0.957)
  Pallas kernels: 79.7 us -> 76.2 us
    pallas_call x1, Pallas kernels: 79.7 us -> 76.2 us  [body(): pl.pallas_call(functools.partial(kernel, nz, ny, nx, nh, stop), out_shape...]
where the time goes in v4:
time: 78 us; the launch traced here: 77.9 us
  Pallas kernels  76.2 us (98%)
  other arithmetic  1.63 us (2%)
    pallas_call x1, Pallas kernels, body(): pl.pallas_call(functools.partial(kernel, nz, ny, nx, nh, stop), out_shape...  76.2 us
    transpose x1, other arithmetic, body(): return edges.astype(f32).reshape(4, listed, tokens).transpose(0, 2, 1)  1.63 us

profile of v4, /device:TPU:8, one launch (start us, length us, event | category | flops | bytes accessed | tf_op | source)
XLA Modules:
  0.0 77.9 jit_solution(6339618419770218971)
XLA Ops:
  0.0 76.2 %shard_map.82 = bf16[2,128,256]{2,1,0:T(8,128)(2,1)} custom-call(s32[32]{0:T(128)} %pos_ref.1, bf16[4,84]{1,0:T(4,128)(2,1)} %grads_ref.1, f32[4,32,256]{2,1,0:T(8,128)} %raw_hbm.1, bf16[84,512]{1,0:T(8,128)(2,1)} %bitcast.9, bf16[84,512]{1,0:T(8,128)(2,1)} %bitcast.10, bf16[384,5376]{1,0:T(8,128)(2,1)} %dec_hbm.1, s32[64,256]{1,0:T(8,128)} %bitcast.11, ...), custom_call_target="tpu_custom_call" | custom-call | tf_op jit(solution)/shard_map/pallas_call | solution.py:431
  76.2 1.6 %convert_bitcast_fusion = f32[4,256,64]{1,2,0:T(8,128)} fusion(bf16[4,64,256]{2,1,0:T(8,128)(2,1)} %bitcast.8), kind=kLoop, calls=%fused_computation | loop fusion | flops 65536 | bytes 393216 | tf_op jit(solution)/shard_map/transpose | solution.py:442

commit v5 on v4

--- a/solution.py
+++ b/solution.py
@@ -19,10 +19,10 @@
 
 def kernel(
     nz, ny, nx, nh, stop,
-    pos_ref, grads_ref, raw_hbm, outp_hbm, valp_hbm, dec_hbm, ids_hbm, act_hbm,
+    pos_hbm, grads_hbm, raw_hbm, outp_hbm, valp_hbm, dec_hbm, ids_hbm, act_hbm,
     out_ref,
-    raw_ref, outp_ref, valp_ref, ids_ref, act_ref, dec, gall, ga, gy, gfull, pall, psend, part, rs, ex, hall, tsend, tall, ax, bx, thr,
-    eparts, ers, e1, eex, fin, pats, ids_t,
+    pos_ref, grads_ref, raw_ref, outp_ref, valp_ref, ids_ref, act_ref, dec, gall, ga, gy, gfull, pall, psend, part, rs, ex, hall, tsend, tall, ax, bx, thr,
+    eparts, ers, e1, eex, pats, ids_t,
     in_sem, ssem, rsem,
 ):
     f32, bf16 = jnp.float32, jnp.bfloat16
@@ -65,11 +65,13 @@
     loads = {}
     for i, (name, src, dst) in enumerate(
         (
+            ("grads", grads_hbm, grads_ref),
             ("raw", raw_hbm, raw_ref),
             ("outp", outp_hbm, outp_ref),
             ("valp", valp_hbm, valp_ref),
             ("ids", ids_hbm, ids_ref),
             ("act", act_hbm, act_ref),
+            ("pos", pos_hbm, pos_ref),
             ("dec", dec_hbm, dec),
         )
     ):
@@ -129,6 +131,7 @@
 
     sent, loaded = [], []
 
+    load("grads")
     own = grads_ref[...].astype(f32)
     mine = jnp.concatenate([own, own], axis=0)
     zero_lanes = jnp.zeros((8, gall.shape[2]), f32)
@@ -157,6 +160,8 @@
     partial += dot(jnp.where(low, 0.0, both).astype(bf16), outp_ref[:, half : 2 * half])
     part[...] = partial.reshape(ny, 8, half)
     c4 = exchange(4, "y", lambda who: part.at[who[1]], lambda d: rs.at[d], rs.at[0 : ny - 1])
+    c1 = exchange(1, "h", lambda who: psend.at[who[3]], lambda d: pall.at[g], pall.at[0 : nh - 1])
+    pall[g] = psend[g]
     c2 = exchange(2, "a", lambda j: ga.at[a], lambda d: ga.at[a], ga.at[0 : na - 1])
 
     arrive(c4)
@@ -251,13 +256,11 @@
     far = {}
     steps = (2, ny - 2, 1, ny - 1) if ny == 8 else (1,)
     for i, d in enumerate(steps):
-        far[d] = send((18, 19 + i if i < 2 and ny == 8 else 18), mine_y, mine_y, y_at(d)[1])
+        far[d] = send((22, 23 + i if i < 2 and ny == 8 else 22), mine_y, mine_y, y_at(d)[1])
     order = (1, ny - 1, 2, ny - 2, 3, ny - 3, 4) if ny == 8 else (1,)
     for d in order:
         cy[d].wait_recv()
         pass_on(d)
-    c1 = exchange(1, "h", lambda who: psend.at[who[3]], lambda d: pall.at[g], pall.at[0 : nh - 1])
-    pall[g] = psend[g]
 
     load("dec")
     arrive(c3)
@@ -265,26 +268,6 @@
         for j in range(ny):
             at = wx * (k * ny + j)
             gfull[0:4, at : at + wx] = gy[j, 4 * k : 4 * k + 4, 0:wx]
-
-    cut = (wx // 32) * 16
-    if ny == 8:
-        far[2].wait_recv()
-        back = thr.at[0, y_at(ny - 2)[0]]
-        far[3] = send((18, 18), back, back, y_at(1)[1])
-        back = thr.at[0, y_at(ny - 2)[0], 0:cut]
-        far["low"] = send((18, 18), back, back, y_at(2)[1])
-        far[ny - 2].wait_recv()
-        back = thr.at[0, y_at(2)[0]]
-        far[ny - 3] = send((18, 18), back, back, y_at(ny - 1)[1])
-        back = thr.at[0, y_at(2)[0], cut:wx]
-        far["high"] = send((18, 18), back, back, y_at(ny - 2)[1])
-    for d in (0,) + order:
-        if d < reach:
-            hops["r", d].wait_recv()
-            send((16, 16), bx.at[from_left, d], bx.at[from_left, d], right)
-        else:
-            hops["l", d].wait_recv()
-            send((16, 17), bx.at[from_right, d], bx.at[from_right, d], left)
 
     arrive(c1)
     raw = pall[...].reshape(rows, tokens)
@@ -293,6 +276,8 @@
     row_pos = jnp.zeros(raw.shape, jnp.int32)
     own_pos = []
     for t in range(4):
+        if t == 0:
+            load("pos")
         own_pos.append(pos_ref[4 * g + t])
         row_pos = jnp.where(row_t == t, own_pos[t], row_pos)
     masked = jnp.where(spot <= row_pos, raw, 0.0)
@@ -303,10 +288,30 @@
     pats[0] = pat_hi
     pats[1] = pat_lo
 
+    cut = (wx // 32) * 16
+    if ny == 8:
+        far[2].wait_recv()
+        back = thr.at[0, y_at(ny - 2)[0]]
+        far[3] = send((22, 22), back, back, y_at(1)[1])
+        back = thr.at[0, y_at(ny - 2)[0], 0:cut]
+        far["low"] = send((22, 22), back, back, y_at(2)[1])
+        far[ny - 2].wait_recv()
+        back = thr.at[0, y_at(2)[0]]
+        far[ny - 3] = send((22, 22), back, back, y_at(ny - 1)[1])
+        back = thr.at[0, y_at(2)[0], cut:wx]
+        far["high"] = send((22, 22), back, back, y_at(ny - 2)[1])
+    for d in (0,) + order:
+        if d < reach:
+            hops["r", d].wait_recv()
+            send((16, 16), bx.at[from_left, d], bx.at[from_left, d], right)
+        else:
+            hops["l", d].wait_recv()
+            send((16, 17), bx.at[from_right, d], bx.at[from_right, d], left)
+
     straight = dot(gfull[...].astype(bf16), dec[...], NT)
 
-    sent.append((18, thr.at[0, 0 : ny - 1]))
-    arrive((18, thr.at[0, 0 : ny - 3] if ny == 8 else thr.at[0, 0 : ny - 1]))
+    sent.append((22, thr.at[0, 0 : ny - 1]))
+    arrive((22, thr.at[0, 0 : ny - 3] if ny == 8 else thr.at[0, 0 : ny - 1]))
     span = ny * wx
     scores = dot(dec[:, 0:span], thr[0].reshape(span, rows))
     sent.extend([(14, bx.at[0]), (15, bx.at[0]), (16, bx.at[0])])
@@ -333,6 +338,7 @@
     of_t = lax.rem(lax.broadcasted_iota(jnp.int32, pat_hi.shape, 1), 4)
     token = lax.broadcasted_iota(jnp.int32, (tokens, feats), 0)
     piece = 2 * listed // ny
+    summed, spread_out, placed = {}, {}, {}
     for p in range(2):
         picked = []
         for q in range(2):
@@ -354,31 +360,52 @@
         edge = jnp.where(lane < listed, picked[0], picked[1]).T * act
         edge = edge.astype(bf16)
         for j in range(ny):
-            eparts[j, p] = edge[piece * j : piece * (j + 1)]
-
-    c10 = exchange(10, "y", lambda who: eparts.at[who[1]], lambda d: ers.at[d], ers.at[0 : ny - 1])
-    arrive(c10)
-    if stop <= 10:
-        return finish()
-    total = eparts[y].astype(f32)
-    for d in range(1, ny):
-        total += ers[d].astype(f32)
-    e1[...] = total.astype(bf16)
-    c11 = exchange(11, "a", lambda j: e1, lambda d: eex.at[d], eex.at[0 : na - 1])
-    arrive(c11)
-    if stop <= 11:
-        return finish()
-    for d in range(1, na):
-        total += eex[d].astype(f32)
-    fin[y] = total.astype(bf16)
-    c12 = exchange(12, "y", lambda j: fin.at[y], lambda d: fin.at[y], fin.at[0 : ny - 1])
-    arrive(c12)
-    if stop <= 12:
-        return finish()
-    for j in range(ny):
-        for p in range(2):
-            out_ref[p, piece * j : piece * (j + 1), :] = fin[j, p]
-
+            eparts[p, j] = edge[piece * j : piece * (j + 1)]
+        summed[p] = exchange(
+            10 if p == 0 else 19,
+            "y",
+            lambda who: eparts.at[p, who[1]],
+            lambda d: ers.at[p, d],
+            ers.at[p, 0 : ny - 1],
+        )
+
+    totals = {}
+    for p in range(2):
+        arrive(summed[p])
+        if stop <= 10 and p == 1:
+            return finish()
+        total = eparts[p, y].astype(f32)
+        for d in range(1, ny):
+            total += ers[p, d].astype(f32)
+        totals[p] = total
+        eex[p, 0] = total.astype(bf16)
+        spread_out[p] = exchange(
+            11 if p == 0 else 20,
+            "a",
+            lambda who: eex.at[p, 0],
+            lambda d: eex.at[p, d],
+            eex.at[p, 0 : na - 1],
+        )
+    keep = {}
+    for p in range(2):
+        arrive(spread_out[p])
+        total = totals[p]
+        for d in range(1, na):
+            total += eex[p, d].astype(f32)
+        e1[p] = total.astype(bf16)
+        mine_out = out_ref.at[p, pl.ds(pl.multiple_of(y * piece, piece), piece), :]
+        placed[p] = exchange(
+            12 if p == 0 else 21,
+            "y",
+            lambda who: e1.at[p],
+            lambda d: mine_out,
+            ers.at[p, 0 : ny - 1],
+        )
+        keep[p] = pltpu.make_async_copy(e1.at[p], mine_out, in_sem.at[p])
+        keep[p].start()
+    for p in range(2):
+        arrive(placed[p])
+        keep[p].wait()
     finish()
 
 
@@ -395,6 +422,8 @@
     tall_w = -(-w // 16) * 16
     vmem = pltpu.VMEM
     scratch = [
+        pltpu.SMEM(positions.shape, jnp.int32),
+        vmem(grads.shape, bf16),
         vmem(raw.shape, f32),
         vmem(out_proj.shape, bf16),
         vmem(value_proj.shape, bf16),
@@ -416,24 +445,21 @@
         vmem((nx, tall_w, rows), bf16),
         vmem((nx, ny, tall_w, rows), bf16),
         vmem((nz, ny, wx, rows), bf16),
-        vmem((ny, 2, piece, tokens), bf16),
-        vmem((ny, 2, piece, tokens), bf16),
+        vmem((2, ny, piece, tokens), bf16),
+        vmem((2, ny, piece, tokens), bf16),
         vmem((2, piece, tokens), bf16),
-        vmem((na, 2, piece, tokens), bf16),
-        vmem((ny, 2, piece, tokens), bf16),
+        vmem((2, na, piece, tokens), bf16),
         vmem((2, tokens, rows), bf16),
         vmem((tokens, 2 * listed), jnp.int32),
-        pltpu.SemaphoreType.DMA((6,)),
-        pltpu.SemaphoreType.DMA((19,)),
+        pltpu.SemaphoreType.DMA((8,)),
+        pltpu.SemaphoreType.DMA((23,)),
         pltpu.SemaphoreType.DMA((32 + ny,)),
     ]
-    in_vmem = pl.BlockSpec(memory_space=pltpu.VMEM)
     edges = pl.pallas_call(
         functools.partial(kernel, nz, ny, nx, nh, stop),
         out_shape=jax.ShapeDtypeStruct((2, 2 * listed, tokens), bf16),
-        in_specs=[pl.BlockSpec(memory_space=pltpu.SMEM), in_vmem]
-        + [pl.BlockSpec(memory_space=pl.ANY)] * 6,
-        out_specs=in_vmem,
+        in_specs=[pl.BlockSpec(memory_space=pl.ANY)] * 8,
+        out_specs=pl.BlockSpec(memory_space=pl.ANY),
         scratch_shapes=scratch,
         compiler_params=pltpu.CompilerParams(
             collective_id=cid, has_side_effects=True, vmem_limit_bytes=60 * 1024 * 1024

time: 78 us -> 76.1 us (0.976)
  Pallas kernels: 76.2 us -> 74.4 us
    pallas_call x1, Pallas kernels: 76.2 us -> 74.4 us  [body(): pl.pallas_call(functools.partial(kernel, nz, ny, nx, nh, stop), out_shape...]
where the time goes in v5:
time: 76.1 us; the launch traced here: 76 us
  Pallas kernels  74.4 us (98%)
  other arithmetic  1.63 us (2%)
    pallas_call x1, Pallas kernels, body(): pl.pallas_call(functools.partial(kernel, nz, ny, nx, nh, stop), out_shape...  74.4 us
    transpose x1, other arithmetic, body(): return edges.astype(f32).reshape(4, listed, tokens).transpose(0, 2, 1)  1.63 us

profile of v5, /device:TPU:8, one launch (start us, length us, event | category | flops | bytes accessed | tf_op | source)
XLA Modules:
  0.0 76.0 jit_solution(17653738621993725192)
XLA Ops:
  0.0 74.4 %shard_map.82 = bf16[2,128,256]{2,1,0:T(8,128)(2,1)} custom-call(s32[32]{0:T(128)} %pos_hbm.1, bf16[4,84]{1,0:T(4,128)(2,1)} %grads_hbm.1, f32[4,32,256]{2,1,0:T(8,128)} %raw_hbm.1, bf16[84,512]{1,0:T(8,128)(2,1)} %bitcast.9, bf16[84,512]{1,0:T(8,128)(2,1)} %bitcast.10, bf16[384,5376]{1,0:T(8,128)(2,1)} %dec_hbm.1, s32[64,256]{1,0:T(8,128)} %bitcast.11, ...), custom_call_target="tpu_custom_call" | custom-call | tf_op jit(solution)/shard_map/pallas_call | solution.py:458
  74.4 1.6 %convert_bitcast_fusion = f32[4,256,64]{1,2,0:T(8,128)} fusion(bf16[4,64,256]{2,1,0:T(8,128)(2,1)} %bitcast.8), kind=kLoop, calls=%fused_computation | loop fusion | flops 65536 | bytes 393216 | tf_op jit(solution)/shard_map/transpose | solution.py:468

commit v6 on v5

--- a/solution.py
+++ b/solution.py
@@ -310,22 +310,21 @@
 
     straight = dot(gfull[...].astype(bf16), dec[...], NT)
 
-    sent.append((22, thr.at[0, 0 : ny - 1]))
-    arrive((22, thr.at[0, 0 : ny - 3] if ny == 8 else thr.at[0, 0 : ny - 1]))
     span = ny * wx
-    scores = dot(dec[:, 0:span], thr[0].reshape(span, rows))
     sent.extend([(14, bx.at[0]), (15, bx.at[0]), (16, bx.at[0])])
     arrive((14, bx.at[0, 0 : ny - reach]))
     arrive((15, bx.at[0, 0:reach]))
     for lane_way, first_d, last_d in ((16, 0, reach), (17, reach, ny)):
         arrive((lane_way, bx.at[0, first_d:last_d]))
-        if stop > 9:
-            for d in range(first_d, last_d):
-                joined = [bx[i, d].astype(f32)[0:w] for i in range(nx)]
-                thr[1, y_at(ny - d)[0]] = jnp.concatenate(joined, axis=0).astype(bf16)
+        for d in range(first_d, last_d):
+            joined = [bx[i, d].astype(f32)[0:w] for i in range(nx)]
+            thr[1, y_at(ny - d)[0]] = jnp.concatenate(joined, axis=0).astype(bf16)
+    scores = dot(dec[:, span : 2 * span], thr[1].reshape(span, rows))
+    sent.append((22, thr.at[0, 0 : ny - 1]))
+    arrive((22, thr.at[0, 0 : ny - 3] if ny == 8 else thr.at[0, 0 : ny - 1]))
     if stop <= 9:
         return finish()
-    scores += dot(dec[:, span : 2 * span], thr[1].reshape(span, rows))
+    scores += dot(dec[:, 0:span], thr[0].reshape(span, rows))
     sc_hi = scores.astype(bf16)
     sc_lo = (scores - sc_hi.astype(f32)).astype(bf16)
     right = jnp.concatenate([sc_hi, sc_hi, sc_lo], axis=1)
@@ -369,16 +368,14 @@
             ers.at[p, 0 : ny - 1],
         )
 
-    totals = {}
     for p in range(2):
         arrive(summed[p])
         if stop <= 10 and p == 1:
             return finish()
-        total = eparts[p, y].astype(f32)
+        total = eparts[p, y]
         for d in range(1, ny):
-            total += ers[p, d].astype(f32)
-        totals[p] = total
-        eex[p, 0] = total.astype(bf16)
+            total += ers[p, d]
+        eex[p, 0] = total
         spread_out[p] = exchange(
             11 if p == 0 else 20,
             "a",
@@ -389,10 +386,10 @@
     keep = {}
     for p in range(2):
         arrive(spread_out[p])
-        total = totals[p]
+        total = eex[p, 0]
         for d in range(1, na):
-            total += eex[p, d].astype(f32)
-        e1[p] = total.astype(bf16)
+            total += eex[p, d]
+        e1[p] = total
         mine_out = out_ref.at[p, pl.ds(pl.multiple_of(y * piece, piece), piece), :]
         placed[p] = exchange(
             12 if p == 0 else 21,
@@ -455,16 +452,20 @@
         pltpu.SemaphoreType.DMA((23,)),
         pltpu.SemaphoreType.DMA((32 + ny,)),
     ]
+    in_hbm = [
+        pltpu.with_memory_space_constraint(array, pltpu.HBM)
+        for array in (positions, grads, raw, out_proj, value_proj, decoders, ids, act)
+    ]
     edges = pl.pallas_call(
         functools.partial(kernel, nz, ny, nx, nh, stop),
         out_shape=jax.ShapeDtypeStruct((2, 2 * listed, tokens), bf16),
-        in_specs=[pl.BlockSpec(memory_space=pl.ANY)] * 8,
-        out_specs=pl.BlockSpec(memory_space=pl.ANY),
+        in_specs=[pl.BlockSpec(memory_space=pltpu.HBM)] * 8,
+        out_specs=pl.BlockSpec(memory_space=pltpu.VMEM),
         scratch_shapes=scratch,
         compiler_params=pltpu.CompilerParams(
-            collective_id=cid, has_side_effects=True, vmem_limit_bytes=60 * 1024 * 1024
+            collective_id=cid, has_side_effects=True, vmem_limit_bytes=24 * 1024 * 1024
         ),
-    )(positions, grads, raw, out_proj, value_proj, decoders, ids, act)
+    )(*in_hbm)
     return edges.astype(f32).reshape(4, listed, tokens).transpose(0, 2, 1)
 
 

time: 76.1 us -> 74.9 us (0.984)
  other arithmetic: 1.63 us -> 0.72 us
    transpose x1, other arithmetic: 1.63 us -> 0.72 us  [body(): return edges.astype(f32).reshape(4, listed, tokens).transpose(0, 2, 1)]
where the time goes in v6:
time: 74.9 us; the launch traced here: 74.8 us
  Pallas kernels  74 us (99%)
    pallas_call x1, Pallas kernels, body(): pl.pallas_call(functools.partial(kernel, nz, ny, nx, nh, stop), out_shape...  74 us

profile of v6, /device:TPU:8, one launch (start us, length us, event | category | flops | bytes accessed | tf_op | source)
XLA Modules:
  0.0 74.8 jit_solution(4142103715364266687)
XLA Ops:
  0.0 74.0 %shard_map.82 = bf16[2,128,256]{2,1,0:T(8,128)(2,1)S(1)} custom-call(s32[32]{0:T(128)} %pos_hbm.1, bf16[4,84]{1,0:T(4,128)(2,1)} %grads_hbm.1, f32[4,32,256]{2,1,0:T(8,128)} %raw_hbm.1, bf16[84,512]{1,0:T(8,128)(2,1)} %bitcast.9, bf16[84,512]{1,0:T(8,128)(2,1)} %bitcast.10, bf16[384,5376]{1,0:T(8,128)(2,1)} %dec_hbm.1, s32[64,256]{1,0:T(8,128)} %bitcast.11, ...), custom_call_target="tpu_custom_call" | custom-call | tf_op jit(solution)/shard_map/pallas_call | solution.py:459
  74.0 0.7 convert_bitcast_fusion

commit v7 on v6

--- a/solution.py
+++ b/solution.py
@@ -113,7 +113,7 @@
         return pltpu.make_async_remote_copy(
             src_ref=whole,
             dst_ref=whole,
-            send_sem=ssem.at[stage],
+            send_sem=ssem.at[min(stage, 22)],
             recv_sem=rsem.at[stage],
             device_id=groups["h"][0][1][4],
             device_id_type=MESH,
@@ -231,7 +231,6 @@
     ax[x] = turned(0)
     cx = exchange(8, "x", lambda j: ax.at[x], lambda d: ax.at[x], ax.at[0 : nx - 1])
     bx[x, 0] = turned(1)
-    cy = exchange(9, "y", lambda j: bx.at[x, 0], lambda d: bx.at[x, d], bx.at[0, 0 : ny - 1], 24)
     right, left = place(0, 0, 1, 0)[4], place(0, 0, nx - 1, 0)[4]
     from_left, from_right = lax.rem(x + nx - 1, nx), lax.rem(x + 1, nx)
 
@@ -239,6 +238,10 @@
         who = place(0, d, 0, 0)
         return who[1], who[4]
 
+    steps = (2, ny - 2, 1, ny - 1) if ny == 8 else (1,)
+    for d in steps:
+        send((9, 24 + d), bx.at[x, 0], bx.at[x, d], y_at(d)[1])
+    sent.append((9, bx.at[0, 0 : ny - 1]))
     hops = {}
     reach = ny // 2
 
@@ -254,12 +257,18 @@
     thr[0, y] = jnp.concatenate(joined, axis=0).astype(bf16)
     mine_y = thr.at[0, y]
     far = {}
-    steps = (2, ny - 2, 1, ny - 1) if ny == 8 else (1,)
     for i, d in enumerate(steps):
         far[d] = send((22, 23 + i if i < 2 and ny == 8 else 22), mine_y, mine_y, y_at(d)[1])
-    order = (1, ny - 1, 2, ny - 2, 3, ny - 3, 4) if ny == 8 else (1,)
+    order = (2, ny - 2, 1, ny - 1, 3, ny - 3, 4) if ny == 8 else (1,)
+    mid = (tall_w // 32) * 16
     for d in order:
-        cy[d].wait_recv()
+        arrive((24 + d, bx.at[0, d]))
+        if d == 2 and ny == 8:
+            send((9, 27), bx.at[x, 2], bx.at[x, 3], y_at(1)[1])
+            send((9, 28), bx.at[x, 2, 0:mid], bx.at[x, 4, 0:mid], y_at(2)[1])
+        if d == ny - 2 and ny == 8:
+            send((9, 29), bx.at[x, 6], bx.at[x, 5], y_at(ny - 1)[1])
+            send((9, 28), bx.at[x, 6, mid:tall_w], bx.at[x, 4, mid:tall_w], y_at(ny - 2)[1])
         pass_on(d)
 
     load("dec")

time: 74.9 us -> 77.9 us (1.040)
  Pallas kernels: 74 us -> 77.1 us
    pallas_call x1, Pallas kernels: 74 us -> 77.1 us  [body(): pl.pallas_call(functools.partial(kernel, nz, ny, nx, nh, stop), out_shape...]
where the time goes in v7:
time: 77.9 us; the launch traced here: 77.8 us
  Pallas kernels  77.1 us (99%)
    pallas_call x1, Pallas kernels, body(): pl.pallas_call(functools.partial(kernel, nz, ny, nx, nh, stop), out_shape...  77.1 us

profile of v7, /device:TPU:8, one launch (start us, length us, event | category | flops | bytes accessed | tf_op | source)
XLA Modules:
  0.0 77.8 jit_solution(5791154346306755966)
XLA Ops:
  0.0 77.1 %shard_map.82 = bf16[2,128,256]{2,1,0:T(8,128)(2,1)S(1)} custom-call(s32[32]{0:T(128)} %pos_hbm.1, bf16[4,84]{1,0:T(4,128)(2,1)} %grads_hbm.1, f32[4,32,256]{2,1,0:T(8,128)} %raw_hbm.1, bf16[84,512]{1,0:T(8,128)(2,1)} %bitcast.9, bf16[84,512]{1,0:T(8,128)(2,1)} %bitcast.10, bf16[384,5376]{1,0:T(8,128)(2,1)} %dec_hbm.1, s32[64,256]{1,0:T(8,128)} %bitcast.11, ...), custom_call_target="tpu_custom_call" | custom-call | tf_op jit(solution)/shard_map/pallas_call | solution.py:468
  77.1 0.7 convert_bitcast_fusion

commit v8 on v6

--- a/solution.py
+++ b/solution.py
@@ -232,21 +232,15 @@
     cx = exchange(8, "x", lambda j: ax.at[x], lambda d: ax.at[x], ax.at[0 : nx - 1])
     bx[x, 0] = turned(1)
     cy = exchange(9, "y", lambda j: bx.at[x, 0], lambda d: bx.at[x, d], bx.at[0, 0 : ny - 1], 24)
-    right, left = place(0, 0, 1, 0)[4], place(0, 0, nx - 1, 0)[4]
-    from_left, from_right = lax.rem(x + nx - 1, nx), lax.rem(x + 1, nx)
-
     def y_at(d):
         who = place(0, d, 0, 0)
         return who[1], who[4]
 
-    hops = {}
-    reach = ny // 2
+    early = (0, 1, ny - 1, 2) if ny == 8 else (0,)
 
     def pass_on(d):
-        sems = (14, 32 + d if d < reach else 14)
-        hops["r", d] = send(sems, bx.at[x, d], bx.at[x, d], right)
-        sems = (15, 32 + d if d >= reach else 15)
-        hops["l", d] = send(sems, bx.at[x, d], bx.at[x, d], left)
+        for slot, who in groups["x"]:
+            send((14, 14 if d in early else 15), bx.at[x, d], bx.at[x, d], who[4])
 
     pass_on(0)
     arrive(cx)
@@ -262,6 +256,18 @@
         cy[d].wait_recv()
         pass_on(d)
 
+    cut = (wx // 32) * 16
+    if ny == 8:
+        far[2].wait_recv()
+        back = thr.at[0, y_at(ny - 2)[0]]
+        far[3] = send((22, 22), back, back, y_at(1)[1])
+        back = thr.at[0, y_at(ny - 2)[0], 0:cut]
+        far["low"] = send((22, 22), back, back, y_at(2)[1])
+        far[ny - 2].wait_recv()
+        back = thr.at[0, y_at(2)[0]]
+        far[ny - 3] = send((22, 22), back, back, y_at(ny - 1)[1])
+        back = thr.at[0, y_at(2)[0], cut:wx]
+        far["high"] = send((22, 22), back, back, y_at(ny - 2)[1])
     load("dec")
     arrive(c3)
     for k in range(nz):
@@ -288,35 +294,14 @@
     pats[0] = pat_hi
     pats[1] = pat_lo
 
-    cut = (wx // 32) * 16
-    if ny == 8:
-        far[2].wait_recv()
-        back = thr.at[0, y_at(ny - 2)[0]]
-        far[3] = send((22, 22), back, back, y_at(1)[1])
-        back = thr.at[0, y_at(ny - 2)[0], 0:cut]
-        far["low"] = send((22, 22), back, back, y_at(2)[1])
-        far[ny - 2].wait_recv()
-        back = thr.at[0, y_at(2)[0]]
-        far[ny - 3] = send((22, 22), back, back, y_at(ny - 1)[1])
-        back = thr.at[0, y_at(2)[0], cut:wx]
-        far["high"] = send((22, 22), back, back, y_at(ny - 2)[1])
-    for d in (0,) + order:
-        if d < reach:
-            hops["r", d].wait_recv()
-            send((16, 16), bx.at[from_left, d], bx.at[from_left, d], right)
-        else:
-            hops["l", d].wait_recv()
-            send((16, 17), bx.at[from_right, d], bx.at[from_right, d], left)
-
     straight = dot(gfull[...].astype(bf16), dec[...], NT)
 
     span = ny * wx
-    sent.extend([(14, bx.at[0]), (15, bx.at[0]), (16, bx.at[0])])
-    arrive((14, bx.at[0, 0 : ny - reach]))
-    arrive((15, bx.at[0, 0:reach]))
-    for lane_way, first_d, last_d in ((16, 0, reach), (17, reach, ny)):
-        arrive((lane_way, bx.at[0, first_d:last_d]))
-        for d in range(first_d, last_d):
+    sent.append((14, bx.at[0 : nx - 1]))
+    late = [d for d in range(ny) if d not in early]
+    for stage, ds in ((14, early), (15, late)):
+        arrive((stage, bx.at[0 : nx - 1, 0 : len(ds)]))
+        for d in ds:
             joined = [bx[i, d].astype(f32)[0:w] for i in range(nx)]
             thr[1, y_at(ny - d)[0]] = jnp.concatenate(joined, axis=0).astype(bf16)
     scores = dot(dec[:, span : 2 * span], thr[1].reshape(span, rows))

time: 74.9 us -> 74.8 us (level)
  no operation moved by 1% of the time
where the time goes in v8:
time: 74.8 us; the launch traced here: 74.7 us
  Pallas kernels  73.9 us (99%)
    pallas_call x1, Pallas kernels, body(): pl.pallas_call(functools.partial(kernel, nz, ny, nx, nh, stop), out_shape...  73.9 us

profile of v8, /device:TPU:8, one launch (start us, length us, event | category | flops | bytes accessed | tf_op | source)
XLA Modules:
  0.0 74.7 jit_solution(6909288797963233215)
XLA Ops:
  0.0 73.9 %shard_map.82 = bf16[2,128,256]{2,1,0:T(8,128)(2,1)S(1)} custom-call(s32[32]{0:T(128)} %pos_hbm.1, bf16[4,84]{1,0:T(4,128)(2,1)} %grads_hbm.1, f32[4,32,256]{2,1,0:T(8,128)} %raw_hbm.1, bf16[84,512]{1,0:T(8,128)(2,1)} %bitcast.9, bf16[84,512]{1,0:T(8,128)(2,1)} %bitcast.10, bf16[384,5376]{1,0:T(8,128)(2,1)} %dec_hbm.1, s32[64,256]{1,0:T(8,128)} %bitcast.11, ...), custom_call_target="tpu_custom_call" | custom-call | tf_op jit(solution)/shard_map/pallas_call | solution.py:444
  73.9 0.7 convert_bitcast_fusion

commit v9 on v8

--- a/solution.py
+++ b/solution.py
@@ -59,9 +59,6 @@
     barrier = pltpu.get_barrier_semaphore()
     greet = groups["a"] + groups["y"] + groups["zh"][1:] + groups["h"]
     greet = [who for slot, who in greet]
-    for who in greet:
-        pl.semaphore_signal(barrier, inc=1, device_id=who[4], device_id_type=MESH)
-
     loads = {}
     for i, (name, src, dst) in enumerate(
         (
@@ -76,7 +73,9 @@
         )
     ):
         loads[name] = pltpu.make_async_copy(src, dst, in_sem.at[i])
-        loads[name].start()
+    loads["grads"].start()
+    for who in greet:
+        pl.semaphore_signal(barrier, inc=1, device_id=who[4], device_id_type=MESH)
 
     def load(name):
         loads[name].wait()
@@ -141,6 +140,10 @@
     ga[a, :, 0:w] = mine
     pl.semaphore_wait(barrier, len(greet))
     c0 = exchange(0, "h", lambda j: gall.at[g], lambda d: gall.at[g], gall.at[0 : nh - 1])
+
+    for name in loads:
+        if name != "grads":
+            loads[name].start()
 
     load("raw")
     for j in range(nh):

time: 74.8 us -> 75 us (level)
  no operation moved by 1% of the time
where the time goes in v9:
time: 75 us; the launch traced here: 74.9 us
  Pallas kernels  74.2 us (99%)
    pallas_call x1, Pallas kernels, body(): pl.pallas_call(functools.partial(kernel, nz, ny, nx, nh, stop), out_shape...  74.2 us

profile of v9, /device:TPU:8, one launch (start us, length us, event | category | flops | bytes accessed | tf_op | source)
XLA Modules:
  0.0 74.9 jit_solution(4654195243310630062)
XLA Ops:
  0.0 74.2 %shard_map.82 = bf16[2,128,256]{2,1,0:T(8,128)(2,1)S(1)} custom-call(s32[32]{0:T(128)} %pos_hbm.1, bf16[4,84]{1,0:T(4,128)(2,1)} %grads_hbm.1, f32[4,32,256]{2,1,0:T(8,128)} %raw_hbm.1, bf16[84,512]{1,0:T(8,128)(2,1)} %bitcast.9, bf16[84,512]{1,0:T(8,128)(2,1)} %bitcast.10, bf16[384,5376]{1,0:T(8,128)(2,1)} %dec_hbm.1, s32[64,256]{1,0:T(8,128)} %bitcast.11, ...), custom_call_target="tpu_custom_call" | custom-call | tf_op jit(solution)/shard_map/pallas_call | solution.py:447
  74.2 0.7 convert_bitcast_fusion

commit v10 on v8

--- a/solution.py
+++ b/solution.py
@@ -222,31 +222,45 @@
     arrive(c7)
     if stop <= 7:
         return finish()
-    tall_w = ax.shape[1]
+    low_w = ax.shape[2]
+    tall_w = 2 * low_w
 
     def turned(k):
         block = tall[k].reshape(rows, tall.shape[3]).astype(f32).T
         return block[0:tall_w].astype(bf16)
 
-    ax[x] = turned(0)
-    cx = exchange(8, "x", lambda j: ax.at[x], lambda d: ax.at[x], ax.at[0 : nx - 1])
-    bx[x, 0] = turned(1)
+    block = turned(0)
+    ax[y, x] = block[0:low_w]
+    cx = exchange(8, "x", lambda j: ax.at[y, x], lambda d: ax.at[y, x], ax.at[0, 0 : nx - 1])
+    bx[x, 0, 0:tall_w] = turned(1)
+    bx[x, 0, tall_w : tall_w + low_w] = block[low_w:tall_w]
     cy = exchange(9, "y", lambda j: bx.at[x, 0], lambda d: bx.at[x, d], bx.at[0, 0 : ny - 1], 24)
     def y_at(d):
         who = place(0, d, 0, 0)
         return who[1], who[4]
 
-    early = (0, 1, ny - 1, 2) if ny == 8 else (0,)
+    hops = {}
+    reach = ny // 2
+    right, left = place(0, 0, 1, 0)[4], place(0, 0, nx - 1, 0)[4]
+    from_left, from_right = lax.rem(x + nx - 1, nx), lax.rem(x + 1, nx)
 
     def pass_on(d):
-        for slot, who in groups["x"]:
-            send((14, 14 if d in early else 15), bx.at[x, d], bx.at[x, d], who[4])
+        sems = (14, 32 + d if d < reach else 14)
+        hops["r", d] = send(sems, bx.at[x, d], bx.at[x, d], right)
+        sems = (15, 32 + d if d >= reach else 15)
+        hops["l", d] = send(sems, bx.at[x, d], bx.at[x, d], left)
+
+    def hand_on(d):
+        if d < reach:
+            hops["r", d].wait_recv()
+            send((16, 16), bx.at[from_left, d], bx.at[from_left, d], right)
+        else:
+            hops["l", d].wait_recv()
+            send((16, 17), bx.at[from_right, d], bx.at[from_right, d], left)
 
     pass_on(0)
     arrive(cx)
-    joined = [ax[i].astype(f32)[0:w] for i in range(nx)]
-    thr[0, y] = jnp.concatenate(joined, axis=0).astype(bf16)
-    mine_y = thr.at[0, y]
+    mine_y = ax.at[y]
     far = {}
     steps = (2, ny - 2, 1, ny - 1) if ny == 8 else (1,)
     for i, d in enumerate(steps):
@@ -255,19 +269,24 @@
     for d in order:
         cy[d].wait_recv()
         pass_on(d)
-
-    cut = (wx // 32) * 16
+    for d in ((0,) + order)[0:4]:
+        hand_on(d)
+
+    cut = nx // 2
     if ny == 8:
         far[2].wait_recv()
-        back = thr.at[0, y_at(ny - 2)[0]]
+        back = ax.at[y_at(ny - 2)[0]]
         far[3] = send((22, 22), back, back, y_at(1)[1])
-        back = thr.at[0, y_at(ny - 2)[0], 0:cut]
+        back = ax.at[y_at(ny - 2)[0], 0:cut]
         far["low"] = send((22, 22), back, back, y_at(2)[1])
         far[ny - 2].wait_recv()
-        back = thr.at[0, y_at(2)[0]]
+        back = ax.at[y_at(2)[0]]
         far[ny - 3] = send((22, 22), back, back, y_at(ny - 1)[1])
-        back = thr.at[0, y_at(2)[0], cut:wx]
+        back = ax.at[y_at(2)[0], cut:nx]
         far["high"] = send((22, 22), back, back, y_at(ny - 2)[1])
+    for d in ((0,) + order)[4:]:
+        hand_on(d)
+
     load("dec")
     arrive(c3)
     for k in range(nz):
@@ -297,18 +316,26 @@
     straight = dot(gfull[...].astype(bf16), dec[...], NT)
 
     span = ny * wx
-    sent.append((14, bx.at[0 : nx - 1]))
-    late = [d for d in range(ny) if d not in early]
-    for stage, ds in ((14, early), (15, late)):
-        arrive((stage, bx.at[0 : nx - 1, 0 : len(ds)]))
+    sent.extend([(14, bx.at[0]), (15, bx.at[0]), (16, bx.at[0])])
+    arrive((14, bx.at[0, 0 : ny - reach]))
+    arrive((15, bx.at[0, 0:reach]))
+    for stage, ds in ((16, range(reach)), (17, range(reach, ny))):
+        arrive((stage, bx.at[0, 0 : len(ds)]))
         for d in ds:
             joined = [bx[i, d].astype(f32)[0:w] for i in range(nx)]
             thr[1, y_at(ny - d)[0]] = jnp.concatenate(joined, axis=0).astype(bf16)
     scores = dot(dec[:, span : 2 * span], thr[1].reshape(span, rows))
-    sent.append((22, thr.at[0, 0 : ny - 1]))
-    arrive((22, thr.at[0, 0 : ny - 3] if ny == 8 else thr.at[0, 0 : ny - 1]))
+    sent.append((22, ax.at[0 : ny - 1]))
+    arrive((22, ax.at[0 : ny - 3] if ny == 8 else ax.at[0 : ny - 1]))
     if stop <= 9:
         return finish()
+    for d in range(ny):
+        at = y_at(ny - d)[0]
+        joined = []
+        for i in range(nx):
+            joined.append(ax[at, i].astype(f32))
+            joined.append(bx[i, d, tall_w : tall_w + low_w].astype(f32)[0 : w - low_w])
+        thr[0, at] = jnp.concatenate(joined, axis=0).astype(bf16)
     scores += dot(dec[:, 0:span], thr[0].reshape(span, rows))
     sc_hi = scores.astype(bf16)
     sc_lo = (scores - sc_hi.astype(f32)).astype(bf16)
@@ -401,7 +428,7 @@
     wx = nx * w
     lanes_w = -(-w // 128) * 128
     lanes_x = -(-wx // 128) * 128
-    tall_w = -(-w // 16) * 16
+    low_w = -(-w // 32) * 16
     vmem = pltpu.VMEM
     scratch = [
         pltpu.SMEM(positions.shape, jnp.int32),
@@ -424,8 +451,8 @@
         vmem((ny, 8, 2 * HD), f32),
         vmem((nh, 16, lanes_w), bf16),
         vmem((nz, nh, 16, lanes_w), bf16),
-        vmem((nx, tall_w, rows), bf16),
-        vmem((nx, ny, tall_w, rows), bf16),
+        vmem((ny, nx, low_w, rows), bf16),
+        vmem((nx, ny, 3 * low_w, rows), bf16),
         vmem((nz, ny, wx, rows), bf16),
         vmem((2, ny, piece, tokens), bf16),
         vmem((2, ny, piece, tokens), bf16),

time: 74.8 us -> 80 us (1.070)
  Pallas kernels: 73.9 us -> 79.2 us
    pallas_call x1, Pallas kernels: 73.9 us -> 79.2 us  [body(): pl.pallas_call(functools.partial(kernel, nz, ny, nx, nh, stop), out_shape...]
where the time goes in v10:
time: 80 us; the launch traced here: 79.9 us
  Pallas kernels  79.2 us (99%)
    pallas_call x1, Pallas kernels, body(): pl.pallas_call(functools.partial(kernel, nz, ny, nx, nh, stop), out_shape...  79.2 us

profile of v10, /device:TPU:8, one launch (start us, length us, event | category | flops | bytes accessed | tf_op | source)
XLA Modules:
  0.0 79.9 jit_solution(9138391868117703092)
XLA Ops:
  0.0 79.2 %shard_map.82 = bf16[2,128,256]{2,1,0:T(8,128)(2,1)S(1)} custom-call(s32[32]{0:T(128)} %pos_hbm.1, bf16[4,84]{1,0:T(4,128)(2,1)} %grads_hbm.1, f32[4,32,256]{2,1,0:T(8,128)} %raw_hbm.1, bf16[84,512]{1,0:T(8,128)(2,1)} %bitcast.9, bf16[84,512]{1,0:T(8,128)(2,1)} %bitcast.10, bf16[384,5376]{1,0:T(8,128)(2,1)} %dec_hbm.1, s32[64,256]{1,0:T(8,128)} %bitcast.11, ...), custom_call_target="tpu_custom_call" | custom-call | tf_op jit(solution)/shard_map/pallas_call | solution.py:471
  79.2 0.7 convert_bitcast_fusion
